TPU v7x, 32 devices: a whole 2x2x4 slice. The times are simulated.
32 devices in a mesh: section: 2 (over y), expert: 8 (over z, x), tensor: 2 (over core).
Axes of the slice: x: 2, y: 2, z: 4, core: 2. Of those that a mesh axis runs over, the one named last changes fastest.
Arguments:
- inputs: float32 [2, 4096, 768], P(None, ('expert', 'tensor')), may hold values from -6 to 6
- cotangent: float32 [2, 4096, 768], P(None, ('expert', 'tensor')), may hold values from -6 to 6
- prev_logits: float32 [2, 2, 4096, 12], P('section', None, ('expert', 'tensor')), may hold values from -3 to 3
- lengths: int32 [2, 8, 4], P(None, 'expert'), may hold values from 1 to 456, 512 in all within a row
- routes: int32 [2, 2, 4096, 2], P('section', None, ('expert', 'tensor')), may hold values from 0 to 11, all different within a row; in each aligned block of 256 rows (0 to 255, 256 to 511, ..., all dimensions but the last counted through in order) at most 98 rows name the same one
- slot_order: int32 [2, 2, 16, 256], P('section', None, ('expert', 'tensor')), may hold values from 0 to 255, each once within a row
- norm_gain1: float32 [2, 768], P('section'), may hold values from 0.5 to 1.5
- w_query: bfloat16 [2, 768, 768], P('section', None, 'tensor'), may hold values from -0.21875 to 0.21875
- w_key: bfloat16 [2, 768, 768], P('section', None, 'tensor'), may hold values from -0.21875 to 0.21875
- w_value: bfloat16 [2, 768, 768], P('section', None, 'tensor'), may hold values from -0.21875 to 0.21875
- w_out: bfloat16 [2, 768, 768], P('section', 'tensor'), may hold values from -0.625 to 0.625
- norm_gain2: float32 [2, 768], P('section'), may hold values from 0.5 to 1.5
- router: float32 [2, 768, 12], P('section'), may hold values from -0.109375 to 0.109375
- router_residual: float32 [2, 12, 12], P('section'), may hold values from -1.75 to 1.75
- const_gate: float32 [2, 2, 768], P('section'), may hold values from -0.21875 to 0.21875
- const_value: float32 [2, 2, 768], P('section'), may hold values from -5 to 5
- expert_gate: bfloat16 [2, 8, 768, 2048], P('section', 'expert', None, 'tensor'), may hold values from -0.21875 to 0.21875
- expert_up: bfloat16 [2, 8, 768, 2048], P('section', 'expert', None, 'tensor'), may hold values from -0.21875 to 0.21875
- expert_down: bfloat16 [2, 8, 2048, 768], P('section', 'expert', 'tensor'), may hold values from -0.125 to 0.125
Outputs:
- layer_outputs: float32 [2, 2, 4096, 768], P('section', None, ('expert', 'tensor'))
- input_grads: float32 [2, 2, 4096, 768], P('section', None, ('expert', 'tensor'))
- logit_grads: float32 [2, 2, 4096, 12], P('section', None, ('expert', 'tensor'))
- norm_gain1_grad: float32 [2, 768], P('section')
- w_query_grad: float32 [2, 768, 768], P('section', None, 'tensor')
- w_key_grad: float32 [2, 768, 768], P('section', None, 'tensor')
- w_value_grad: float32 [2, 768, 768], P('section', None, 'tensor')
- w_out_grad: float32 [2, 768, 768], P('section', 'tensor')
- norm_gain2_grad: float32 [2, 768], P('section')
- router_grad: float32 [2, 768, 12], P('section')
- router_residual_grad: float32 [2, 12, 12], P('section')
- const_gate_grad: float32 [2, 2, 768], P('section')
- const_value_grad: float32 [2, 2, 768], P('section')
- expert_gate_grad: float32 [2, 8, 768, 2048], P('section', 'expert', None, 'tensor')
- expert_up_grad: float32 [2, 8, 768, 2048], P('section', 'expert', None, 'tensor')
- expert_down_grad: float32 [2, 8, 2048, 768], P('section', 'expert', 'tensor')
Inputs may be any that keep to these rules, and one draw needn't show every extreme that they name: In each micro-batch and block, the first 3 entries are the lengths of the sequences packed in order into the block's 512 rows and the last is the number of padding rows at its end; the entries sum to 512 and the largest is exactly 456. `routes`: each row names two different choices: 0 to 7 are feed-forward experts, 8 the zero expert, 9 the copy expert, 10 and 11 the constant experts. Within the 256 rows of one device no choice is named by more than 98 rows, and every choice is named somewhere. `slot_order`: for each layer, micro-batch and device, a permutation of 0 to 256 - 1 over the device's rows.
All inputs are finite; a program needn't handle non-finite values.
Results may differ from a plain program's by a relative error of at most 0.028.
Values may be sent and summed in bfloat16 or wider, within the bound.
A program may use at most 256 MiB of HBM per device.

v0:
```python
import jax
import jax.numpy as jnp
from jax import lax
from jax.sharding import PartitionSpec as P

HEAD_DIM = 64


epsilon = 1e-06
highest = lax.Precision.HIGHEST


def passed_along(value, axis, steps):
    count = lax.axis_size(axis)
    initial, last = (max(0, -steps), min(count, count - steps))
    return lax.ppermute(value, axis, [(source, source + steps) for source in range(initial, last)])


def normed(values, gain):
    return values * lax.rsqrt(jnp.mean(values * values, axis=-1, keepdims=True) + epsilon) * gain


def layout(lengths_row, row_count, seq_count):
    seq_ends = jnp.cumsum(lengths_row)
    row_index = jnp.arange(row_count, dtype=jnp.int32)
    passed = row_index[:, None] >= seq_ends[None, :seq_count]
    segment = jnp.sum(passed.astype(jnp.int32), axis=1)
    seq_start = jnp.sum(jnp.where(passed, lengths_row[None, :seq_count], 0), axis=1)
    return (row_index - seq_start, segment)


def block_mask(segment, block_rows, seq_count):
    key_index = jnp.arange(segment.shape[0], dtype=jnp.int32)
    query_index = jnp.arange(block_rows, dtype=jnp.int32)
    same_seq = segment[:, None] == segment[None, :]
    causal = key_index[None, :] <= query_index[:, None]
    own_rows = (segment[:, None] < seq_count) | (key_index[None, :] == query_index[:, None])
    return same_seq & causal & own_rows


def rotary(values, position):
    half_width = values.shape[-1] // 2
    frequency = 10000.0 ** (-2.0 * jnp.arange(half_width, dtype=jnp.float32) / values.shape[-1])
    angles = position.astype(jnp.float32)[:, None] * frequency[None, :]
    cosine = jnp.cos(angles)[:, None, :]
    sine_part = jnp.sin(angles)[:, None, :]
    leading = values[..., :half_width]
    trailing = values[..., half_width:]
    return jnp.concatenate(
        [leading * cosine - trailing * sine_part, trailing * cosine + leading * sine_part], axis=-1
    )


def dot_plain(left, right):
    return jnp.dot(left, right, preferred_element_type=jnp.float32)


def dot_leading(left, right):
    return lax.dot_general(
        left, right, (((0,), (0,)), ((), ())), preferred_element_type=jnp.float32
    )


def dot_trailing(left, right):
    return lax.dot_general(
        left, right, (((1,), (1,)), ((), ())), preferred_element_type=jnp.float32
    )


def dot_exact(left, right):
    return jnp.dot(left, right, precision=highest)


def gather_rows(values):
    return lax.all_gather(values, "tensor", axis=0, tiled=True)


def gather_grad_rows(values):
    return lax.all_gather(values, "tensor", axis=0, tiled=True)


def sum_rows(source, weight, owned):

    def partial_term(row_start, row_count):
        return dot_plain(source, weight)

    return lax.psum_scatter(
        partial_term(jnp.int32(0), lax.axis_size("tensor") * owned).astype(jnp.bfloat16),
        "tensor",
        scatter_dimension=0,
        tiled=True,
    ).astype(jnp.float32)


def sum_grad_rows(sources, weights, owned):

    def partial_term(row_start, row_count):
        summed = dot_trailing(sources[0], weights[0])
        for source, weight in zip(sources[1:], weights[1:]):
            summed = summed + dot_trailing(source, weight)
        return summed

    return lax.psum_scatter(
        partial_term(jnp.int32(0), lax.axis_size("tensor") * owned).astype(jnp.bfloat16),
        "tensor",
        scatter_dimension=0,
        tiled=True,
    ).astype(jnp.float32)


def dispatch_slots(values):
    return lax.all_to_all(values, "expert", split_axis=0, concat_axis=0, tiled=True)


def return_slots(values):
    return lax.all_to_all(values, "expert", split_axis=0, concat_axis=0, tiled=True)


def dispatch_grads(values):
    return lax.all_to_all(values, "expert", split_axis=0, concat_axis=0, tiled=True)


def return_grads(values):
    return lax.all_to_all(values, "expert", split_axis=0, concat_axis=0, tiled=True)


def pass_forward(values):
    return passed_along(values.astype(jnp.bfloat16), "section", 1).astype(values.dtype)


def pass_backward(values):
    return passed_along(values.astype(jnp.bfloat16), "section", -1).astype(values.dtype)


def stack_all(*pieces):
    return jnp.stack(pieces)


def local(
    inputs,
    cotangent,
    prev_logits,
    lengths,
    routes,
    slot_order,
    norm_gain1,
    w_query,
    w_key,
    w_value,
    w_out,
    norm_gain2,
    router,
    router_residual,
    const_gate,
    const_value,
    expert_gate,
    expert_up,
    expert_down,
):
    sections = lax.axis_size("section")
    tensors = lax.axis_size("tensor")
    sources = lax.axis_size("expert")
    section_rank = lax.axis_index("section")
    micro_count = inputs.shape[0]
    owned = inputs.shape[1]
    model_width = inputs.shape[2]
    seq_rows = owned * tensors
    seq_count = lengths.shape[2] - 1
    choices = router.shape[2]
    experts = choices - 4
    capacity = 9 * 2 * owned // (8 * choices) + 1
    dump_slot = experts * capacity
    slot_rows = sources * capacity
    heads_local = w_query.shape[2] // HEAD_DIM
    scale_factor = HEAD_DIM ** (-0.5)
    block_size = seq_rows
    while block_size > 1024 and block_size % 2 == 0:
        block_size = block_size // 2
    tick_count = micro_count + sections - 1
    gain_one = norm_gain1[0]
    query_weight = w_query[0]
    key_weight = w_key[0]
    value_weight = w_value[0]
    out_weight = w_out[0]
    gain_two = norm_gain2[0]
    router_weight = router[0]
    residual_weight = router_residual[0]
    mix_gate = const_gate[0]
    mix_value = const_value[0]
    gate_weight = expert_gate[0, 0]
    up_weight = expert_up[0, 0]
    down_weight = expert_down[0, 0]

    def expert_backward(kept_rows, arrived_grads):
        all_grads = gather_grad_rows(arrived_grads)
        gate_matrix, up_matrix, down_matrix = (gate_weight, up_weight, down_weight)
        gate_value = dot_plain(kept_rows, gate_matrix)
        up_value = dot_plain(kept_rows, up_matrix)
        sigmoid_gate = jax.nn.sigmoid(gate_value)
        activated = gate_value * sigmoid_gate
        hidden = (activated * up_value).astype(jnp.bfloat16)
        down_grad = dot_leading(hidden, all_grads)
        hidden_grad = dot_trailing(all_grads, down_matrix)
        gate_grad = (
            hidden_grad * up_value * sigmoid_gate * (1.0 + gate_value * (1.0 - sigmoid_gate))
        ).astype(jnp.bfloat16)
        up_grad = (hidden_grad * activated).astype(jnp.bfloat16)
        gate_weight_grad = dot_leading(kept_rows, gate_grad)
        up_weight_grad = dot_leading(kept_rows, up_grad)
        slot_input_grad = sum_grad_rows(
            (gate_grad, up_grad), (gate_matrix, up_matrix), slot_rows
        ).astype(jnp.bfloat16)
        return (slot_input_grad, gate_weight_grad, up_weight_grad, down_grad)

    def make_onehot(route_rows):
        return (
            route_rows[:, :, None] == jnp.arange(choices, dtype=jnp.int32)[None, None, :]
        ).astype(jnp.float32)

    def branches(normed_wide, onehot, back_padded, destination):
        mix_rate = jax.nn.sigmoid(dot_exact(normed_wide, mix_gate.T))
        mix_out = (
            mix_rate[:, :, None] * normed_wide[:, None, :]
            + (1.0 - mix_rate)[:, :, None] * mix_value[None, :, :]
        )
        branch = (
            back_padded[destination].astype(jnp.float32)
            + onehot[:, :, experts + 1, None] * normed_wide[:, None, :]
        )
        branch = (
            branch
            + onehot[:, :, experts + 2, None] * mix_out[:, None, 0, :]
            + onehot[:, :, experts + 3, None] * mix_out[:, None, 1, :]
        )
        return (branch, mix_rate)

    def layer_backward(kept, grad_out, prev_rows, lengths_row, route_rows):
        (
            x_rows,
            hidden_state,
            normed_full,
            query_rot,
            key_rot,
            values,
            mixed,
            log_total,
            normed_two,
            gates,
            destination,
            slot_token,
            kept_rows,
            back_padded,
        ) = kept
        position, segment = layout(lengths_row, seq_rows, seq_count)
        normed_wide = normed_two.astype(jnp.float32)
        onehot = make_onehot(route_rows)
        branch, mix_rate = branches(normed_wide, onehot, back_padded, destination)
        gate_grads = jnp.sum(grad_out[:, None, :] * branch, axis=2)
        coupled = gates[:, 0] * gates[:, 1] * (gate_grads[:, 0] - gate_grads[:, 1])
        logit_grad = coupled[:, None] * (onehot[:, 0, :] - onehot[:, 1, :])
        router_grad = dot_exact(normed_wide.T, logit_grad)
        residual_grad = dot_exact(prev_rows.T, logit_grad)
        prev_grad = dot_exact(logit_grad, residual_weight.T)
        normed_grad = dot_exact(logit_grad, router_weight.T)
        branch_grad = gates[:, :, None] * grad_out[:, None, :]
        normed_grad = normed_grad + jnp.sum(onehot[:, :, experts + 1, None] * branch_grad, axis=1)
        mix_grad = (
            onehot[:, 0, experts + 2 :, None] * branch_grad[:, 0, None, :]
            + onehot[:, 1, experts + 2 :, None] * branch_grad[:, 1, None, :]
        )
        normed_grad = normed_grad + jnp.sum(mix_rate[:, :, None] * mix_grad, axis=1)
        rate_grad = jnp.sum(mix_grad * (normed_wide[:, None, :] - mix_value[None, :, :]), axis=2)
        logit_mix = rate_grad * mix_rate * (1.0 - mix_rate)
        normed_grad = normed_grad + dot_exact(logit_mix, mix_gate)
        mix_gate_grad = dot_exact(logit_mix.T, normed_wide)
        mix_value_grad = jnp.sum((1.0 - mix_rate)[:, :, None] * mix_grad, axis=0)
        slot_weight = (
            jnp.zeros((dump_slot + 1,), jnp.float32)
            .at[destination.reshape(-1)]
            .set(gates.reshape(-1))[:dump_slot]
        )
        grad_padded = jnp.concatenate([grad_out, jnp.zeros((1, model_width), jnp.float32)], axis=0)
        slot_grads = (grad_padded[slot_token] * slot_weight[:, None]).astype(jnp.bfloat16)
        arrived_grads = dispatch_grads(slot_grads.reshape(experts, capacity, model_width)).reshape(
            slot_rows, model_width
        )
        slot_input_grad, gate_weight_grad, up_weight_grad, down_weight_grad = expert_backward(
            kept_rows, arrived_grads
        )
        back_grads = return_grads(slot_input_grad.reshape(sources, capacity, model_width)).reshape(
            dump_slot, model_width
        )
        back_grads = jnp.concatenate(
            [back_grads, jnp.zeros((1, model_width), jnp.bfloat16)], axis=0
        )
        normed_grad = normed_grad + jnp.sum(back_grads[destination].astype(jnp.float32), axis=1)
        unused_two, pull_two = jax.vjp(normed, hidden_state, gain_two)
        state_grad, gain_two_grad = pull_two(normed_grad)
        state_grad = grad_out + state_grad
        attn_full = gather_grad_rows(state_grad.astype(jnp.bfloat16))
        out_weight_grad = dot_leading(mixed, attn_full)
        mixed_grad = (
            dot_trailing(attn_full, out_weight)
            .astype(jnp.bfloat16)
            .reshape(seq_rows, heads_local, HEAD_DIM)
        )
        scores = (
            jnp.einsum("qhd,khd->hqk", query_rot, key_rot, preferred_element_type=jnp.float32)
            * scale_factor
        )
        scores = jnp.where(block_mask(segment, block_size, seq_count)[None], scores, -1e30)
        probability = jnp.exp(scores - log_total)
        prob_grad = jnp.einsum(
            "qhd,khd->hqk", mixed_grad, values, preferred_element_type=jnp.float32
        )
        score_grad = (
            probability * (prob_grad - jnp.sum(prob_grad * probability, axis=-1, keepdims=True))
        ).astype(jnp.bfloat16)
        query_parts = (
            jnp.einsum("hqk,khd->qhd", score_grad, key_rot, preferred_element_type=jnp.float32)
            * scale_factor
        )
        key_grad = (
            jnp.einsum("hqk,qhd->khd", score_grad, query_rot, preferred_element_type=jnp.float32)
            * scale_factor
        )
        value_grad = jnp.einsum(
            "hqk,qhd->khd",
            probability.astype(jnp.bfloat16),
            mixed_grad,
            preferred_element_type=jnp.float32,
        )
        zeros_rot = jnp.zeros((seq_rows, heads_local, HEAD_DIM), jnp.float32)
        unused_rot, unrotate = jax.vjp(lambda rotated_in: rotary(rotated_in, position), zeros_rot)
        query_back = (
            unrotate(query_parts)[0].reshape(seq_rows, heads_local * HEAD_DIM).astype(jnp.bfloat16)
        )
        key_back = (
            unrotate(key_grad)[0].reshape(seq_rows, heads_local * HEAD_DIM).astype(jnp.bfloat16)
        )
        value_back = value_grad.reshape(seq_rows, heads_local * HEAD_DIM).astype(jnp.bfloat16)
        query_weight_grad = dot_leading(normed_full, query_back)
        key_weight_grad = dot_leading(normed_full, key_back)
        value_weight_grad = dot_leading(normed_full, value_back)
        normed_one_grad = sum_grad_rows(
            (query_back, key_back, value_back), (query_weight, key_weight, value_weight), owned
        )
        unused_one, pull_one = jax.vjp(normed, x_rows, gain_one)
        input_part, gain_one_grad = pull_one(normed_one_grad)
        grads_layer = (
            gain_one_grad,
            query_weight_grad,
            key_weight_grad,
            value_weight_grad,
            out_weight_grad,
            gain_two_grad,
            router_grad,
            residual_grad,
            mix_gate_grad,
            mix_value_grad,
            gate_weight_grad,
            up_weight_grad,
            down_weight_grad,
        )
        return (state_grad + input_part, prev_grad, grads_layer)

    is_first = section_rank == 0
    is_last = section_rank == sections - 1
    received = jnp.zeros((owned, model_width), jnp.float32)
    layer_outputs = jnp.zeros((micro_count, owned, model_width), jnp.float32)
    kept_list = []
    for tick_index in range(tick_count):
        offset = tick_index - section_rank
        micro_index = jnp.clip(offset, 0, micro_count - 1)
        active = (offset >= 0) & (offset < micro_count)
        block_input = jnp.where(is_first, inputs[min(tick_index, micro_count - 1)], received)
        layer_route_rows = routes[0, micro_index]
        order_row = slot_order[0, micro_index, 0]
        layer_position, layer_segment = layout(lengths[micro_index, 0], seq_rows, seq_count)
        normed_one = normed(block_input, gain_one).astype(jnp.bfloat16)
        layer_normed_full = gather_rows(normed_one)
        query_pre = dot_plain(layer_normed_full, query_weight).reshape(
            seq_rows, heads_local, HEAD_DIM
        )
        key_pre = dot_plain(layer_normed_full, key_weight).reshape(seq_rows, heads_local, HEAD_DIM)
        layer_query_rot = rotary(query_pre, layer_position).astype(jnp.bfloat16)
        layer_key_rot = rotary(key_pre, layer_position).astype(jnp.bfloat16)
        layer_values = (
            dot_plain(layer_normed_full, value_weight)
            .astype(jnp.bfloat16)
            .reshape(seq_rows, heads_local, HEAD_DIM)
        )
        layer_scores = (
            jnp.einsum(
                "qhd,khd->hqk", layer_query_rot, layer_key_rot, preferred_element_type=jnp.float32
            )
            * scale_factor
        )
        layer_scores = jnp.where(
            block_mask(layer_segment, block_size, seq_count)[None], layer_scores, -1e30
        )
        row_peak = jnp.max(layer_scores, axis=-1, keepdims=True)
        shifted = jnp.exp(layer_scores - row_peak)
        totals = jnp.sum(shifted, axis=-1, keepdims=True)
        weights_soft = (shifted / totals).astype(jnp.bfloat16)
        mixed_parts = jnp.einsum(
            "hqk,khd->qhd", weights_soft, layer_values, preferred_element_type=jnp.float32
        ).astype(jnp.bfloat16)
        log_parts = row_peak + jnp.log(totals)
        layer_mixed = mixed_parts.reshape(seq_rows, heads_local * HEAD_DIM)
        layer_hidden_state = block_input + sum_rows(layer_mixed, out_weight, owned)
        layer_normed_two = normed(layer_hidden_state, gain_two).astype(jnp.bfloat16)
        layer_normed_wide = layer_normed_two.astype(jnp.float32)
        logits = dot_exact(layer_normed_wide, router_weight) + dot_exact(
            prev_logits[0, micro_index], residual_weight
        )
        layer_onehot = make_onehot(layer_route_rows)
        picked = jnp.sum(logits[:, None, :] * layer_onehot, axis=2)
        shifted_two = jnp.exp(picked - jnp.max(picked, axis=1, keepdims=True))
        layer_gates = shifted_two / jnp.sum(shifted_two, axis=1, keepdims=True)
        before = (order_row[None, :] < order_row[:, None]).astype(jnp.bfloat16)
        earlier = dot_plain(before, jnp.sum(layer_onehot, axis=1).astype(jnp.bfloat16))
        slot_index = jnp.sum(earlier[:, None, :] * layer_onehot, axis=2).astype(jnp.int32)
        kept_route = (layer_route_rows < experts) & (slot_index < capacity)
        layer_destination = jnp.where(
            kept_route, layer_route_rows * capacity + slot_index, dump_slot
        )
        token_index = jnp.broadcast_to(jnp.arange(owned, dtype=jnp.int32)[:, None], (owned, 2))
        layer_slot_token = (
            jnp.full((dump_slot + 1,), owned, jnp.int32)
            .at[layer_destination.reshape(-1)]
            .set(token_index.reshape(-1))[:dump_slot]
        )
        padded = jnp.concatenate(
            [layer_normed_two, jnp.zeros((1, model_width), jnp.bfloat16)], axis=0
        )
        layer_arrived = dispatch_slots(
            padded[layer_slot_token].reshape(experts, capacity, model_width)
        ).reshape(slot_rows, model_width)
        everyone = gather_rows(layer_arrived)
        expert_gate_value = dot_plain(everyone, gate_weight)
        expert_up_value = dot_plain(everyone, up_weight)
        expert_hidden = (
            expert_gate_value * jax.nn.sigmoid(expert_gate_value) * expert_up_value
        ).astype(jnp.bfloat16)
        result = sum_rows(expert_hidden, down_weight, slot_rows).astype(jnp.bfloat16)
        came_back = return_slots(result.reshape(sources, capacity, model_width)).reshape(
            dump_slot, model_width
        )
        layer_back_padded = jnp.concatenate(
            [came_back, jnp.zeros((1, model_width), jnp.bfloat16)], axis=0
        )
        layer_branch, layer_mix_rate = branches(
            layer_normed_wide, layer_onehot, layer_back_padded, layer_destination
        )
        layer_out = layer_hidden_state + jnp.sum(layer_gates[:, :, None] * layer_branch, axis=1)
        layer_kept = (
            block_input,
            layer_hidden_state,
            layer_normed_full,
            layer_query_rot,
            layer_key_rot,
            layer_values,
            layer_mixed,
            log_parts,
            layer_normed_two,
            layer_gates,
            layer_destination,
            layer_slot_token,
            everyone,
            layer_back_padded,
        )
        layer_out, kept = (layer_out, layer_kept)
        layer_outputs = layer_outputs.at[micro_index].set(
            jnp.where(active, layer_out, layer_outputs[micro_index])
        )
        kept_list.append(kept)
        if tick_index + 1 < tick_count:
            received = pass_forward(layer_out)
    kept_all = jax.tree.map(stack_all, *kept_list)
    grad_totals = None
    received = jnp.zeros((owned, model_width), jnp.float32)
    input_grads = jnp.zeros((micro_count, owned, model_width), jnp.float32)
    logit_grads = jnp.zeros((micro_count, owned, choices), jnp.float32)
    for tick_index in range(tick_count):
        offset = tick_index - (sections - 1 - section_rank)
        micro_index = jnp.clip(offset, 0, micro_count - 1)
        active = (offset >= 0) & (offset < micro_count)
        grad_out = jnp.where(is_last, cotangent[micro_index], received)
        stash_index = jnp.clip(micro_index + section_rank, 0, tick_count - 1)
        kept = jax.tree.map(lambda stacked: stacked[stash_index], kept_all)
        input_rows_grad, prev_grad, grads_layer = layer_backward(
            kept,
            grad_out,
            prev_logits[0, micro_index],
            lengths[micro_index, 0],
            routes[0, micro_index],
        )
        masked = jax.tree.map(lambda value_in: jnp.where(active, value_in, 0.0), grads_layer)
        if grad_totals is None:
            grad_totals = masked
        else:
            grad_totals = jax.tree.map(jnp.add, grad_totals, masked)
        input_grads = input_grads.at[micro_index].set(
            jnp.where(active, input_rows_grad, input_grads[micro_index])
        )
        logit_grads = logit_grads.at[micro_index].set(
            jnp.where(active, prev_grad, logit_grads[micro_index])
        )
        if tick_index + 1 < tick_count:
            received = pass_backward(input_rows_grad)
    (
        gain_one_grad,
        query_weight_grad,
        key_weight_grad,
        value_weight_grad,
        out_weight_grad,
        gain_two_grad,
        router_grad,
        residual_grad,
        mix_gate_grad,
        mix_value_grad,
        gate_weight_grad,
        up_weight_grad,
        down_weight_grad,
    ) = grad_totals
    query_weight_grad, key_weight_grad, value_weight_grad, out_weight_grad = lax.psum(
        (query_weight_grad, key_weight_grad, value_weight_grad, out_weight_grad), "expert"
    )
    gain_one_grad, gain_two_grad, router_grad, residual_grad, mix_gate_grad, mix_value_grad = (
        lax.psum(
            (
                gain_one_grad,
                gain_two_grad,
                router_grad,
                residual_grad,
                mix_gate_grad,
                mix_value_grad,
            ),
            ("expert", "tensor"),
        )
    )
    return (
        layer_outputs[None],
        input_grads[None],
        logit_grads[None],
        gain_one_grad[None],
        query_weight_grad[None],
        key_weight_grad[None],
        value_weight_grad[None],
        out_weight_grad[None],
        gain_two_grad[None],
        router_grad[None],
        residual_grad[None],
        mix_gate_grad[None],
        mix_value_grad[None],
        gate_weight_grad[None, None],
        up_weight_grad[None, None],
        down_weight_grad[None, None],
    )


def solution(mesh):
    in_specs = (
        P(None, ("expert", "tensor"), None),
        P(None, ("expert", "tensor"), None),
        P("section", None, ("expert", "tensor"), None),
        P(None, "expert", None),
        P("section", None, ("expert", "tensor"), None),
        P("section", None, ("expert", "tensor"), None),
        P("section", None),
        P("section", None, "tensor"),
        P("section", None, "tensor"),
        P("section", None, "tensor"),
        P("section", "tensor", None),
        P("section", None),
        P("section", None, None),
        P("section", None, None),
        P("section", None, None),
        P("section", None, None),
        P("section", "expert", None, "tensor"),
        P("section", "expert", None, "tensor"),
        P("section", "expert", "tensor", None),
    )
    out_specs = (
        P("section", None, ("expert", "tensor"), None),
        P("section", None, ("expert", "tensor"), None),
        P("section", None, ("expert", "tensor"), None),
        P("section", None),
        P("section", None, "tensor"),
        P("section", None, "tensor"),
        P("section", None, "tensor"),
        P("section", "tensor", None),
        P("section", None),
        P("section", None, None),
        P("section", None, None),
        P("section", None, None),
        P("section", None, None),
        P("section", "expert", None, "tensor"),
        P("section", "expert", None, "tensor"),
        P("section", "expert", "tensor", None),
    )
    return jax.shard_map(local, mesh=mesh, in_specs=in_specs, out_specs=out_specs, check_vma=False)
```

profile of v0, /device:TPU:10, one launch (start us, length us, event | category | flops | bytes accessed | tf_op | source)
XLA Modules:
  0.0 1149.3 jit_solution(10366707719320963827)
XLA Ops:
  34.9 7.1 reduce-scatter.13.cloned.1.call-done
  56.6 22.7 %all_to_all.60 = bf16[8,49,768]{2,1,0:T(8,128)(2,1)} all-to-all(bf16[8,49,768]{2,1,0:T(8,128)(2,1)} %reshape.2793), channel_id=1, replica_groups=mesh['section'=2,'expert'=8,'tensor'=2] {'expert'}, dimensions={0} | all-to-all | bytes 1204224 | tf_op jit(solution)/shard_map/all_to_all | solution.py:112
  81.5 10.0 all-gather.7.cloned.1.call-done
  91.5 4.4 fusion.69
  95.9 7.0 fusion.74
  104.6 8.4 reduce-scatter.15.cloned.1.call-done
  115.1 6.0 all-to-all-start.1
  127.0 9.2 all-to-all-done.1
  146.1 5.1 multiply_reduce_fusion.20
  155.2 8.2 collective-permute-done
  179.9 9.5 reduce-scatter.17.cloned.1.call-done
  202.1 6.2 all-to-all-start.2
  210.3 13.2 %all-to-all-done.2 = bf16[8,49,768]{2,1,0:T(8,128)(2,1)S(1)} async-done(((bf16[8,49,768]{2,1,0:T(8,128)(2,1)}), bf16[8,49,768]{2,1,0:T(8,128)(2,1)S(1)}, u32[]{:S(2)}, u32[]{:S(2)}) %all-to-all-start.2) | async-done | bytes 602144 | tf_op jit(solution)/shard_map/all_to_all | solution.py:112
  227.0 9.0 all-gather.9.cloned.1.call-done
  235.9 4.5 fusion.67
  240.4 7.0 fusion.77
  273.4 6.0 all-to-all-start.3
  288.9 5.8 all-to-all-done.3
  304.5 5.1 multiply_reduce_fusion.19
  310.5 4.2 collective-permute-start.1
  372.1 7.0 all-to-all-start.4
  399.6 7.5 all-to-all-start.6
  424.9 4.4 fusion.65
  429.3 7.0 fusion.80
  447.4 5.4 multiply_convert_fusion.11
  458.7 5.5 multiply_add_fusion.1
  468.4 6.0 all-to-all-start.5
  483.2 6.0 all-to-all-done.5
  490.0 6.9 all-to-all-start.7
  508.7 15.2 %multiply_reduce_fusion.5 = (f32[2,768]{1,0:T(2,128)}, f32[256,2]{1,0:T(8,128)}, f32[256,768]{1,0:T(8,128)}, f32[256,768]{1,0:T(8,128)}, f32[256,2]{1,0:T(8,128)S(1)}) fusion(f32[256,768]{1,0:T(8,128)} %get-tuple-element.533, f32[256,2]{1,0:T(8,128)} %copy.519, f32[256,768]{1,0:T(8,128)} %get-tuple-element.534, f32[256,2]{1,0:T(8,128)} %copy.518, ...), kind=kLoop, calls=%fused_computation.135 | loop fusion | flops 7861760 | bytes 7897088 | tf_op jit(solution)/shard_map/reduce_sum | solution.py:276
  533.6 4.2 reduce_sum.766
  548.2 4.6 fusion.113
  552.9 5.9 multiply_reduce_fusion.2
  558.8 4.7 multiply_convert_fusion.2
  576.5 3.7 fusion.354
  596.7 8.7 collective-permute-done.2
  613.7 6.1 all-to-all-start.8
  637.7 5.0 fusion.44
  653.2 5.6 multiply_convert_fusion.9
  663.0 5.0 fusion.40
  668.0 4.0 fusion.24
  685.3 6.3 all-to-all-start.9
  691.7 15.8 %multiply_reduce_fusion.4 = (f32[2,768]{1,0:T(2,128)}, f32[256,2]{1,0:T(8,128)}, f32[256,768]{1,0:T(8,128)}, f32[256,768]{1,0:T(8,128)}, f32[256,2]{1,0:T(8,128)}) fusion(f32[256,768]{1,0:T(8,128)} %bitcast.1150, f32[256,2]{1,0:T(8,128)} %copy.536, f32[256,768]{1,0:T(8,128)} %bitcast.1151, f32[256,2]{1,0:T(8,128)} %copy.535, f32[256,2]{1,0:T(8,128)} %copy.532, ...), kind=kLoop, calls=%fused_computation.134 | loop fusion | flops 7861760 | bytes 7897088 | tf_op jit(solution)/shard_map/reduce_sum | solution.py:276
  734.1 4.6 fusion.116
  738.8 5.9 multiply_reduce_fusion.1
  744.6 4.7 multiply_convert_fusion.1
  799.4 6.2 all-to-all-start.10
  812.9 7.7 all-to-all-done.10
  822.8 5.4 fusion.129
  828.3 4.0 fusion.25
  838.6 5.7 multiply_convert_fusion.7
  848.5 5.4 fusion.131
  872.6 6.0 all-to-all-start.11
  878.7 18.9 %multiply_reduce_fusion.3 = (f32[2,768]{1,0:T(2,128)}, f32[256,2]{1,0:T(8,128)}, f32[256,768]{1,0:T(8,128)}, f32[256,768]{1,0:T(8,128)}, f32[256,2]{1,0:T(8,128)S(1)}, /*index=5*/f32[256,2,768]{2,1,0:T(2,128)}) fusion(f32[256,768]{1,0:T(8,128)} %bitcast.1145, f32[256,2]{1,0:T(8,128)} %copy.553, f32[256,768]{1,0:T(8,128)} %bitcast.1148, f32[256,2]{1,0:T(8,128)} %copy.552, ...), kind=kLoop, calls=%fused_computation.133 | loop fusion | flops 9041408 | bytes 10260480 | tf_op jit(solution)/shard_map/reduce_sum | solution.py:276
  911.4 4.2 reduce_sum.790
  925.1 4.6 fusion.119
  929.8 5.8 multiply_reduce_fusion
  935.6 4.7 multiply_convert_fusion
  968.3 5.2 multiply_reduce_fusion.18
  974.5 6.6 add_bitcast_fusion.1
  981.2 3.8 add_bitcast_fusion.2
  987.5 4.3 add_bitcast_fusion
  995.3 54.6 %all-reduce.24 = (f32[1,768]{1,0:T(1,128)}, f32[1,768]{1,0:T(1,128)}, f32[1,768,12]{1,2,0:T(8,128)}, f32[1,12,12]{2,1,0:T(8,128)}, f32[1,2,768]{2,1,0:T(2,128)}, /*index=5*/f32[1,2,768]{2,1,0:T(2,128)}) all-reduce(f32[1,768]{1,0:T(1,128)S(1)} %broadcast_in_dim.274, ...), channel_id=1, replica_groups=mesh['section'=2,'expert'=8,'tensor'=2] {'expert','tensor'}, use_global_device_ids=true, to_apply=%region_105.106 | all-reduce | flops 13968 | bytes 111744 | tf_op jit(solution)/shard_map/psum | solution.py:531
  1056.4 79.1 %all-reduce.28.cloned.1.call-done = (f32[1,768,384]{2,1,0:T(8,128)}, f32[1,768,384]{2,1,0:T(8,128)}, f32[1,768,384]{2,1,0:T(8,128)}, f32[1,384,768]{2,1,0:T(8,128)}) async-done(((f32[1,768,384]{2,1,0:T(8,128)}, f32[1,768,384]{2,1,0:T(8,128)}, f32[1,768,384]{2,1,0:T(8,128)}, f32[1,384,768]{2,1,0:T(8,128)}), (f32[1,768,384]{2,1,0:T(8,128)}, f32[1,768,384]{2,1,0:T(8,128)}, f32[1,768,384]{2,1,0:T(8,128)}, ...) | async-done | bytes 4718608 | tf_op jit(solution)/shard_map/psum | solution.py:527
  (1370 shorter events, 573.0 us)
Async XLA Ops:
  7.2 84.3 %copy-start = (bf16[1,1,768,1024]{3,2,1,0:T(8,128)(2,1)S(1)}, bf16[1,1,768,1024]{3,2,1,0:T(8,128)(2,1)}, u32[]{:S(2)}) copy-start(bf16[1,1,768,1024]{3,2,1,0:T(8,128)(2,1)} %param.53) | copy-start | bytes 4718596
  7.2 34.9 %reduce-scatter.13.cloned.1.call-start = ((), (), s32[]{:S(2)}) async-start(), calls=%async_computation.24 | async-start | bytes 1179648 | tf_op jit(solution)/shard_map/reduce_scatter | solution.py:87
  14.0 137.2 %copy-start.3 = (f32[1,256,768]{2,1,0:T(8,128)}, f32[1,256,768]{2,1,0:T(8,128)S(1)}, u32[]{:S(2)}) copy-start(f32[1,256,768]{2,1,0:T(8,128)S(1)} %get-tuple-element.330) | copy-start | bytes 2359300
  32.3 59.2 %all-gather.7.cloned.1.call-start = ((), (), s32[]{:S(2)}) async-start(), calls=%async_computation.25 | async-start | bytes 1806336 | tf_op jit(solution)/shard_map/all_gather | solution.py:75
  32.6 323.5 %copy-start.219 = (f32[768]{0:T(1024)}, f32[768]{0:T(1024)S(1)}, u32[]{:S(2)}) copy-start(f32[768]{0:T(1024)S(1)} %reduce.49) | copy-start | bytes 9220
  45.6 58.3 %copy-start.54 = (bf16[256,768]{1,0:T(8,128)(2,1)}, bf16[256,768]{1,0:T(8,128)(2,1)S(1)}, u32[]{:S(2)}) copy-start(bf16[256,768]{1,0:T(8,128)(2,1)S(1)} %get-tuple-element.328) | copy-start | bytes 1179652
  47.0 79.9 %copy-start.130 = (f32[256,2]{1,0:T(8,128)}, f32[256,2]{1,0:T(8,128)S(1)}, u32[]{:S(2)}) copy-start(f32[256,2]{1,0:T(8,128)S(1)} %get-tuple-element.277) | copy-start | bytes 6148
  81.4 31.5 %reduce-scatter.15.cloned.1.call-start = ((), (), s32[]{:S(2)}) async-start(), calls=%async_computation.26 | async-start | bytes 1806336 | tf_op jit(solution)/shard_map/reduce_scatter | solution.py:87
  103.8 17.5 %copy-start.247 = (f32[1,2,768]{2,1,0:T(2,128)S(1)}, f32[1,2,768]{2,1,0:T(2,128)}, u32[]{:S(2)}) copy-start(f32[1,2,768]{2,1,0:T(2,128)} %param.52) | copy-start | bytes 18436
  115.1 21.2 %all-to-all-start.1 = ((bf16[8,49,768]{2,1,0:T(8,128)(2,1)}), bf16[8,49,768]{2,1,0:T(8,128)(2,1)}, u32[]{:S(2)}, u32[]{:S(2)}) async-start(bf16[8,49,768]{2,1,0:T(8,128)(2,1)} %reshape.2795), calls=%async_computation.3 | async-start | bytes 1376256 | tf_op jit(solution)/shard_map/all_to_all | solution.py:116
  121.1 68.4 %reduce-scatter.17.cloned.1.call-start = ((), (), s32[]{:S(2)}) async-start(), calls=%async_computation.27 | async-start | bytes 1179648 | tf_op jit(solution)/shard_map/reduce_scatter | solution.py:87
  151.4 12.1 %collective-permute-start = (bf16[256,768]{1,0:T(8,128)(2,1)S(1)}, bf16[256,768]{1,0:T(8,128)(2,1)S(1)}, u32[]{:S(2)}, u32[]{:S(2)}) collective-permute-start(bf16[256,768]{1,0:T(8,128)(2,1)S(1)} %add_convert_fusion.19), channel_id=1, source_target_pairs={{0,16},{1,17},{2,18},{3,19},{4,20},{5,21},{6,22},{7,23},{8,24},{9,... | collective-permute-start | bytes 1179656 | tf_op jit(solution)/shard_map/ppermute | solution.py:16
  202.1 21.4 %all-to-all-start.2 = ((bf16[8,49,768]{2,1,0:T(8,128)(2,1)}), bf16[8,49,768]{2,1,0:T(8,128)(2,1)S(1)}, u32[]{:S(2)}, u32[]{:S(2)}) async-start(bf16[8,49,768]{2,1,0:T(8,128)(2,1)} %reshape.2801), calls=%async_computation.5 | async-start | bytes 1376256 | tf_op jit(solution)/shard_map/all_to_all | solution.py:112
  208.2 27.7 %all-gather.9.cloned.1.call-start = ((), (), s32[]{:S(2)}) async-start(), calls=%async_computation.28 | async-start | bytes 1806336 | tf_op jit(solution)/shard_map/all_gather | solution.py:75
  208.9 152.1 %copy-start.77 = (s32[1,1,256,2]{3,2,1,0:T(8,128)}, s32[1,1,256,2]{3,2,1,0:T(8,128)S(1)}, u32[]{:S(2)}) copy-start(s32[1,1,256,2]{3,2,1,0:T(8,128)S(1)} %copy.614) | copy-start | bytes 6148
  208.9 15.8 %copy-start.360 = (s32[3]{0:T(128)S(1)}, s32[3]{0:T(128)}, u32[]{:S(2)}) copy-start(s32[3]{0:T(128)} %constant.269.clone.1) | copy-start | bytes 40
  208.9 17.4 %copy-start.272 = (f32[6,512]{1,0:T(8,128)S(1)}, f32[6,512]{1,0:T(8,128)}, u32[]{:S(2)}) copy-start(f32[6,512]{1,0:T(8,128)} %copy-done.271) | copy-start | bytes 36868
  208.9 17.4 %copy-start.274 = (f32[6,512]{1,0:T(8,128)S(1)}, f32[6,512]{1,0:T(8,128)}, u32[]{:S(2)}) copy-start(f32[6,512]{1,0:T(8,128)} %copy-done.273) | copy-start | bytes 36868
  210.2 50.8 %copy-start.41 = (f32[256,768]{1,0:T(8,128)}, f32[256,768]{1,0:T(8,128)S(1)}, u32[]{:S(2)}) copy-start(f32[256,768]{1,0:T(8,128)S(1)} %select_bitcast_fusion) | copy-start | bytes 2359300
  210.2 30.2 %copy-start.256 = (f32[256,2,12]{0,2,1:T(8,128)}, f32[256,2,12]{0,2,1:T(8,128)S(1)}, u32[]{:S(2)}) copy-start(f32[256,2,12]{0,2,1:T(8,128)S(1)} %fusion.451) | copy-start | bytes 73732
  210.3 30.1 %copy-start.254 = (f32[256,2,12]{0,2,1:T(8,128)}, f32[256,2,12]{0,2,1:T(8,128)S(1)}, u32[]{:S(2)}) copy-start(f32[256,2,12]{0,2,1:T(8,128)S(1)} %fusion.452) | copy-start | bytes 73732
  224.5 46.8 %reduce-scatter.19.cloned.1.call-start = ((), (), s32[]{:S(2)}) async-start(), calls=%async_computation.29 | async-start | bytes 1806336 | tf_op jit(solution)/shard_map/reduce_scatter | solution.py:87
  273.4 21.2 %all-to-all-start.3 = ((bf16[8,49,768]{2,1,0:T(8,128)(2,1)}), bf16[8,49,768]{2,1,0:T(8,128)(2,1)}, u32[]{:S(2)}, u32[]{:S(2)}) async-start(bf16[8,49,768]{2,1,0:T(8,128)(2,1)} %reshape.2803), calls=%async_computation.7 | async-start | bytes 1376256 | tf_op jit(solution)/shard_map/all_to_all | solution.py:116
  279.5 74.5 %reduce-scatter.21.cloned.1.call-start = ((), (), s32[]{:S(2)}) async-start(), calls=%async_computation.30 | async-start | bytes 1179648 | tf_op jit(solution)/shard_map/reduce_scatter | solution.py:87
  310.5 12.4 %collective-permute-start.1 = (bf16[256,768]{1,0:T(8,128)(2,1)}, bf16[256,768]{1,0:T(8,128)(2,1)}, u32[]{:S(2)}, u32[]{:S(2)}) collective-permute-start(bf16[256,768]{1,0:T(8,128)(2,1)} %add_convert_fusion.18), channel_id=1, source_target_pairs={{0,16},{1,17},{2,18},{3,19},{4,20},{5,21},{6,22},{7,23},{8,24},{9,... | collective-permute-start | bytes 1179656 | tf_op jit(solution)/shard_map/ppermute | solution.py:16
  359.5 19.7 %copy-start.307 = (f32[256]{0:T(256)}, f32[256]{0:T(256)S(1)}, u32[]{:S(2)}) copy-start(f32[256]{0:T(256)S(1)} %reduce_max.59) | copy-start | bytes 3076
  363.6 15.5 %copy-start.325 = (f32[256]{0:T(256)}, f32[256]{0:T(256)S(1)}, u32[]{:S(2)}) copy-start(f32[256]{0:T(256)S(1)} %fusion.433) | copy-start | bytes 3076
  372.1 22.1 %all-to-all-start.4 = ((bf16[8,49,768]{2,1,0:T(8,128)(2,1)}), bf16[8,49,768]{2,1,0:T(8,128)(2,1)}, u32[]{:S(2)}, u32[]{:S(2)}) async-start(bf16[8,49,768]{2,1,0:T(8,128)(2,1)} %reshape.2809), calls=%async_computation.9 | async-start | bytes 1376256 | tf_op jit(solution)/shard_map/all_to_all | solution.py:112
  379.1 45.8 %all-gather.11.cloned.1.call-start = ((), (), s32[]{:S(2)}) async-start(), calls=%async_computation.31 | async-start | bytes 1806336 | tf_op jit(solution)/shard_map/all_gather | solution.py:75
  389.8 29.8 %copy-start.10 = (bf16[3,256,768]{2,1,0:T(8,128)(2,1)}, bf16[3,256,768]{2,1,0:T(8,128)(2,1)S(1)}, u32[]{:S(2)}) copy-start(bf16[3,256,768]{2,1,0:T(8,128)(2,1)S(1)} %pad_maximum_fusion.5) | copy-start | bytes 3538948
  397.4 18.5 %copy-start.25 = (f32[256,768]{1,0:T(8,128)S(1)}, f32[256,768]{1,0:T(8,128)}, u32[]{:S(2)}) copy-start(f32[256,768]{1,0:T(8,128)} %copy-done.23) | copy-start | bytes 2359300
  399.6 23.0 %all-to-all-start.6 = ((bf16[8,49,768]{2,1,0:T(8,128)(2,1)}), bf16[8,49,768]{2,1,0:T(8,128)(2,1)}, u32[]{:S(2)}, u32[]{:S(2)}) async-start(bf16[8,49,768]{2,1,0:T(8,128)(2,1)} %multiply_convert_fusion.20), calls=%async_computation.12 | async-start | bytes 1376256 | tf_op jit(solution)/shard_map/all_to_all | solution.py:120
  407.1 36.8 %all-gather.13.cloned.1.call-start = ((), (), s32[]{:S(2)}) async-start(), calls=%async_computation.33 | async-start | bytes 1806336 | tf_op jit(solution)/shard_map/all_gather | solution.py:79
  420.9 37.8 %copy-start.75 = (f32[256,768]{1,0:T(8,128)}, f32[256,768]{1,0:T(8,128)S(1)}, u32[]{:S(2)}) copy-start(f32[256,768]{1,0:T(8,128)S(1)} %get-tuple-element.369) | copy-start | bytes 2359300
  424.8 41.4 %reduce-scatter.23.cloned.1.call-start = ((), (), s32[]{:S(2)}) async-start(), calls=%async_computation.32 | async-start | bytes 1806336 | tf_op jit(solution)/shard_map/reduce_scatter | solution.py:87
  436.3 44.7 %reduce-scatter.25.cloned.1.call-start = ((), (), s32[]{:S(2)}) async-start(), calls=%async_computation.34 | async-start | bytes 1806336 | tf_op jit(solution)/shard_map/reduce_scatter | solution.py:103
  468.4 20.7 %all-to-all-start.5 = ((bf16[8,49,768]{2,1,0:T(8,128)(2,1)}), bf16[8,49,768]{2,1,0:T(8,128)(2,1)S(1)}, u32[]{:S(2)}, u32[]{:S(2)}) async-start(bf16[8,49,768]{2,1,0:T(8,128)(2,1)} %reshape.2811), calls=%async_computation.11 | async-start | bytes 1376256 | tf_op jit(solution)/shard_map/all_to_all | solution.py:116
  490.0 35.8 %all-to-all-start.7 = ((bf16[8,49,768]{2,1,0:T(8,128)(2,1)}), bf16[8,49,768]{2,1,0:T(8,128)(2,1)S(1)}, u32[]{:S(2)}, u32[]{:S(2)}) async-start(bf16[8,49,768]{2,1,0:T(8,128)(2,1)} %reshape.2815), calls=%async_computation.14 | async-start | bytes 1376256 | tf_op jit(solution)/shard_map/all_to_all | solution.py:124
  496.9 90.5 %reduce-scatter.27.cloned.1.call-start = ((), (), s32[]{:S(2)}) async-start(), calls=%async_computation.35 | async-start | bytes 1179648 | tf_op jit(solution)/shard_map/reduce_scatter | solution.py:103
  508.7 16.4 %copy-start.259 = (f32[256,2,12]{0,2,1:T(8,128)S(1)}, f32[256,2,12]{0,2,1:T(8,128)}, u32[]{:S(2)}) copy-start(f32[256,2,12]{0,2,1:T(8,128)} %copy-done.258) | copy-start | bytes 73732
  525.0 15.1 %copy-start.298 = (f32[256,2]{0,1:T(2,128)}, f32[256,2]{0,1:T(2,128)S(1)}, u32[]{:S(2)}) copy-start(f32[256,2]{0,1:T(2,128)S(1)} %copy.520) | copy-start | bytes 6148
  552.8 16.2 %copy-start.165 = (bf16[6,64,512]{2,1,0:T(8,128)(2,1)}, bf16[6,64,512]{2,1,0:T(8,128)(2,1)S(1)}, u32[]{:S(2)}) copy-start(bf16[6,64,512]{2,1,0:T(8,128)(2,1)S(1)} %fusion.113) | copy-start | bytes 1179652
  591.9 13.5 %collective-permute-start.2 = (bf16[256,768]{1,0:T(8,128)(2,1)S(1)}, bf16[256,768]{1,0:T(8,128)(2,1)S(1)}, u32[]{:S(2)}, u32[]{:S(2)}) collective-permute-start(bf16[256,768]{1,0:T(8,128)(2,1)S(1)} %fusion.585), channel_id=1, source_target_pairs={{16,0},{17,1},{18,2},{19,3},{20,4},{21,5},{22,6},{23,7},{24,8},{25... | collective-permute-start | bytes 1179656 | tf_op jit(solution)/shard_map/ppermute | solution.py:16
  613.7 21.8 %all-to-all-start.8 = ((bf16[8,49,768]{2,1,0:T(8,128)(2,1)}), bf16[8,49,768]{2,1,0:T(8,128)(2,1)}, u32[]{:S(2)}, u32[]{:S(2)}) async-start(bf16[8,49,768]{2,1,0:T(8,128)(2,1)} %multiply_convert_fusion.19), calls=%async_computation.16 | async-start | bytes 1376256 | tf_op jit(solution)/shard_map/all_to_all | solution.py:120
  619.8 30.0 %all-gather.15.cloned.1.call-start = ((), (), s32[]{:S(2)}) async-start(), calls=%async_computation.36 | async-start | bytes 1806336 | tf_op jit(solution)/shard_map/all_gather | solution.py:79
  637.6 45.6 %reduce-scatter.29.cloned.1.call-start = ((), (), s32[]{:S(2)}) async-start(), calls=%async_computation.37 | async-start | bytes 1806336 | tf_op jit(solution)/shard_map/reduce_scatter | solution.py:103
  685.3 27.5 %all-to-all-start.9 = ((bf16[8,49,768]{2,1,0:T(8,128)(2,1)}), bf16[8,49,768]{2,1,0:T(8,128)(2,1)}, u32[]{:S(2)}, u32[]{:S(2)}) async-start(bf16[8,49,768]{2,1,0:T(8,128)(2,1)} %reshape.2821), calls=%async_computation.18 | async-start | bytes 1376256 | tf_op jit(solution)/shard_map/all_to_all | solution.py:124
  691.7 78.1 %reduce-scatter.31.cloned.1.call-start = ((), (), s32[]{:S(2)}) async-start(), calls=%async_computation.38 | async-start | bytes 1179648 | tf_op jit(solution)/shard_map/reduce_scatter | solution.py:103
  691.7 18.0 %copy-start.257 = (f32[256,2,12]{0,2,1:T(8,128)S(1)}, f32[256,2,12]{0,2,1:T(8,128)}, u32[]{:S(2)}) copy-start(f32[256,2,12]{0,2,1:T(8,128)} %copy-done.256) | copy-start | bytes 73732
  708.5 16.5 %copy-start.302 = (f32[256,2]{0,1:T(2,128)}, f32[256,2]{0,1:T(2,128)S(1)}, u32[]{:S(2)}) copy-start(f32[256,2]{0,1:T(2,128)S(1)} %copy.537) | copy-start | bytes 6148
  738.7 17.1 %copy-start.166 = (bf16[6,64,512]{2,1,0:T(8,128)(2,1)}, bf16[6,64,512]{2,1,0:T(8,128)(2,1)S(1)}, u32[]{:S(2)}) copy-start(bf16[6,64,512]{2,1,0:T(8,128)(2,1)S(1)} %fusion.116) | copy-start | bytes 1179652
  775.7 16.6 %collective-permute-start.3 = (bf16[256,768]{1,0:T(8,128)(2,1)}, bf16[256,768]{1,0:T(8,128)(2,1)S(1)}, u32[]{:S(2)}, u32[]{:S(2)}) collective-permute-start(bf16[256,768]{1,0:T(8,128)(2,1)} %fusion.584), channel_id=1, source_target_pairs={{16,0},{17,1},{18,2},{19,3},{20,4},{21,5},{22,6},{23,7},{24,8},{25... | collective-permute-start | bytes 1179656 | tf_op jit(solution)/shard_map/ppermute | solution.py:16
  799.4 21.2 %all-to-all-start.10 = ((bf16[8,49,768]{2,1,0:T(8,128)(2,1)}), bf16[8,49,768]{2,1,0:T(8,128)(2,1)}, u32[]{:S(2)}, u32[]{:S(2)}) async-start(bf16[8,49,768]{2,1,0:T(8,128)(2,1)} %multiply_convert_fusion.18), calls=%async_computation.20 | async-start | bytes 1376256 | tf_op jit(solution)/shard_map/all_to_all | solution.py:120
  805.6 29.6 %all-gather.17.cloned.1.call-start = ((), (), s32[]{:S(2)}) async-start(), calls=%async_computation.39 | async-start | bytes 1806336 | tf_op jit(solution)/shard_map/all_gather | solution.py:79
  809.7 18.5 %copy-start.232 = (f32[2,256,12]{1,2,0:T(8,128)}, f32[2,256,12]{1,2,0:T(8,128)S(1)}, u32[]{:S(2)}) copy-start(f32[2,256,12]{1,2,0:T(8,128)S(1)} %fusion.156) | copy-start | bytes 73732
  822.7 47.7 %reduce-scatter.33.cloned.1.call-start = ((), (), s32[]{:S(2)}) async-start(), calls=%async_computation.40 | async-start | bytes 1806336 | tf_op jit(solution)/shard_map/reduce_scatter | solution.py:103
  872.6 29.9 %all-to-all-start.11 = ((bf16[8,49,768]{2,1,0:T(8,128)(2,1)}), bf16[8,49,768]{2,1,0:T(8,128)(2,1)}, u32[]{:S(2)}, u32[]{:S(2)}) async-start(bf16[8,49,768]{2,1,0:T(8,128)(2,1)} %reshape.2827), calls=%async_computation.22 | async-start | bytes 1376256 | tf_op jit(solution)/shard_map/all_to_all | solution.py:124
  878.6 113.8 %reduce-scatter.35.cloned.1.call-start = ((), (), s32[]{:S(2)}) async-start(), calls=%async_computation.41 | async-start | bytes 1179648 | tf_op jit(solution)/shard_map/reduce_scatter | solution.py:103
  878.7 20.7 %copy-start.255 = (f32[256,2,12]{0,2,1:T(8,128)S(1)}, f32[256,2,12]{0,2,1:T(8,128)}, u32[]{:S(2)}) copy-start(f32[256,2,12]{0,2,1:T(8,128)} %copy-done.254) | copy-start | bytes 73732
  899.4 56.9 %copy-start.216 = (f32[256,12]{0,1:T(8,128)}, f32[256,12]{0,1:T(8,128)S(1)}, u32[]{:S(2)}) copy-start(f32[256,12]{0,1:T(8,128)S(1)} %fusion.502) | copy-start | bytes 36868
  929.7 17.1 %copy-start.168 = (bf16[6,64,512]{2,1,0:T(8,128)(2,1)}, bf16[6,64,512]{2,1,0:T(8,128)(2,1)S(1)}, u32[]{:S(2)}) copy-start(bf16[6,64,512]{2,1,0:T(8,128)(2,1)S(1)} %fusion.119) | copy-start | bytes 1179652
  948.6 186.9 %all-reduce.28.cloned.1.call-start = ((), (), s32[]{:S(2)}) async-start(), calls=%async_computation.42 | async-start | bytes 9437184 | tf_op jit(solution)/shard_map/psum | solution.py:527
  987.5 65.8 %copy-start.34 = (f32[2,256,768]{2,1,0:T(8,128)S(1)}, f32[2,256,768]{2,1,0:T(8,128)}, u32[]{:S(2)}) copy-start(f32[2,256,768]{2,1,0:T(8,128)} %copy-done.33) | copy-start | bytes 4718596
  992.4 60.8 %copy-start.164 = (bf16[256,768]{1,0:T(8,128)(2,1)S(1)}, bf16[256,768]{1,0:T(8,128)(2,1)}, u32[]{:S(2)}) copy-start(bf16[256,768]{1,0:T(8,128)(2,1)} %reduce-scatter.35.cloned.1.call-done) | copy-start | bytes 1179652
  (368 other events, 1468.0 us)
Sparse Core Ops, SparseCore 0:
  32.4 9.6 reduce-scatter.12
  81.5 9.9 all-gather.6
  103.0 9.8 reduce-scatter.14
  178.0 11.3 reduce-scatter.16
  224.6 11.2 all-gather.8
  247.5 9.8 reduce-scatter.18
  338.2 11.3 reduce-scatter.20
  396.4 12.3 all-gather.10
  424.9 11.3 all-gather.12
  438.6 9.8 reduce-scatter.22
  457.1 11.0 reduce-scatter.24
  571.0 10.7 reduce-scatter.26
  637.7 9.4 all-gather.14
  663.1 8.9 reduce-scatter.28
  757.7 8.4 reduce-scatter.30
  822.9 12.3 all-gather.16
  848.6 9.8 reduce-scatter.32
  948.7 9.3 reduce-scatter.34
  964.8 170.6 all-reduce.27
where the time goes:
time: 1170 us; the launch traced here: 1150 us
  local copies, waits for them, and re-layouts  275 us (24%)
  matrix products  271 us (23%)
  other arithmetic  216 us (18%)
  waiting for transfers between devices  191 us (16%)
  blocking collectives  93.7 us (8%)
  starting transfers between devices  82.6 us (7%)
  between operations  19.4 us (2%)
    psum x1, waiting for transfers between devices, local(): lax.psum((query_weight_grad, key_weight_grad, value_weight_grad, out_weig...  79.1 us
    dot_general x27, matrix products, dot_plain(): return jnp.dot(left, right, preferred_element_type=jnp.float32)  76.1 us
    unnamed x827, local copies, waits for them, and re-layouts  67.2 us
    dot_general x21, matrix products, dot_leading(): lax.dot_general(left, right, (((0,), (0,)), ((), ())), preferred_element_...  64.4 us
    psum x1, blocking collectives, local(): lax.psum((gain_one_grad, gain_two_grad, router_grad, residual_grad, mix_g...  54.6 us
    reduce_sum x3, other arithmetic, layer_backward(): mix_value_grad = jnp.sum((1.0 - mix_rate)[:, :, None] * mix_grad, axis=0)  50 us
    dot_general x30, matrix products, dot_exact(): return jnp.dot(left, right, precision=highest)  36.5 us
    dot_general x21, matrix products, dot_trailing(): lax.dot_general(left, right, (((1,), (1,)), ((), ())), preferred_element_...  31.5 us
  transfers between devices with their start and end apart: 34, of which 16 were waited for; matrix products, arithmetic and copies ran while one was open for 35% of the time, Pallas kernels for 0%

commit v1 on v0

v1 whole, which is shorter than its diff:
```python
import functools
import types

import jax
import jax.numpy as jnp
import numpy as np
from jax import lax
from jax.experimental import pallas as pl
from jax.experimental.pallas import tpu as pltpu
from jax.sharding import PartitionSpec as P

HEAD_DIM = 64
LANES = 128
EPSILON = 1e-06
MESH = pl.DeviceIdType.MESH
f32, bf16, i32 = jnp.float32, jnp.bfloat16, jnp.int32

P_NORM, P_OUT, P_ROWS, P_PART, P_GROWS, P_GPART, P_DA, P_DX = range(8)


def dot(left, right):
    return jnp.dot(left, right, preferred_element_type=f32)


def dot_nt(left, right):
    return lax.dot_general(left, right, (((1,), (1,)), ((), ())), preferred_element_type=f32)


def dot_tn(left, right):
    return lax.dot_general(left, right, (((0,), (0,)), ((), ())), preferred_element_type=f32)


def wide(values):
    return values.astype(f32)


def halves(values):
    upper = values.astype(bf16)
    return upper, (values - wide(upper)).astype(bf16)


def dot3(how, left, right):
    left_hi, left_lo = halves(left)
    right_hi, right_lo = halves(right)
    return how(left_hi, right_hi) + (how(left_hi, right_lo) + how(left_lo, right_hi))


def inverse_rms(values):
    return lax.rsqrt(jnp.mean(values * values, axis=-1, keepdims=True) + EPSILON)


def iota(shape, dim):
    return lax.broadcasted_iota(i32, shape, dim)


def flag(condition):
    return wide(condition.astype(i32))


def half_lanes(width):
    return (iota((1, width), 1) % HEAD_DIM) < HEAD_DIM // 2


def turned(values, cosine, sine):
    quarter = HEAD_DIM // 2
    other = jnp.where(
        half_lanes(LANES),
        -pltpu.roll(values, LANES - quarter, 1),
        pltpu.roll(values, quarter, 1),
    )
    return values * cosine + other * sine


def turned_back(values, cosine, sine):
    quarter = HEAD_DIM // 2
    other = jnp.where(
        half_lanes(LANES),
        pltpu.roll(values, LANES - quarter, 1),
        -pltpu.roll(values, quarter, 1),
    )
    return values * cosine + other * sine


def chain_kernel(cfg, names, *refs):
    r = types.SimpleNamespace(**dict(zip(names, refs, strict=True)))
    owned, rows, experts, cap, cap_pad = cfg.owned, cfg.rows, cfg.experts, cfg.cap, cfg.cap_pad
    choices, slots, tiles, tile_rows = cfg.choices, cfg.slots, cfg.tiles, cfg.tile_rows
    per_tile, micro, sections, seqs = cfg.per_tile, cfg.micro, cfg.sections, cfg.seqs
    pairs, chunk = cfg.heads // 2, cfg.chunk
    scale = HEAD_DIM ** (-0.5)
    sec, me, core = (lax.axis_index(a) for a in ("section", "expert", "tensor"))
    other = 1 - core
    own_rows = pl.ds(pl.multiple_of(core * owned, owned), owned)
    other_rows = pl.ds(pl.multiple_of(other * owned, owned), owned)
    is_first, is_last = sec == 0, sec == sections - 1

    def pair(kind, m, j, source, target):
        return pltpu.make_async_remote_copy(
            src_ref=source,
            dst_ref=target,
            send_sem=r.pair_send.at[kind, m, j],
            recv_sem=r.pair_recv.at[kind, m, j],
            device_id={"tensor": other},
            device_id_type=MESH,
        )

    def hop(kind, m, source, target, section):
        return pltpu.make_async_remote_copy(
            src_ref=source,
            dst_ref=target,
            send_sem=r.hop_send.at[kind, m],
            recv_sem=r.hop_recv.at[kind, m],
            device_id={"section": section},
            device_id_type=MESH,
        )

    def slot_rows(index):
        return pl.ds(pl.multiple_of(index * cap_pad, cap_pad), cap_pad)

    def tile_of(j):
        return pl.ds(pl.multiple_of(j * tile_rows, tile_rows), tile_rows)

    def exchange(kind, m, peer, landed, source, target):
        return pltpu.make_async_remote_copy(
            src_ref=source.at[slot_rows(peer)],
            dst_ref=target.at[slot_rows(landed)],
            send_sem=r.a2a_send.at[kind, m, peer],
            recv_sem=r.a2a_recv.at[kind, m, landed],
            device_id={"expert": peer},
            device_id_type=MESH,
        )

    def send_all(kind, m, source, target):
        def step(k, carry):
            exchange(kind, m, lax.rem(me + k, experts), me, source, target).start()
            return carry

        lax.fori_loop(1, experts, step, 0)

    def wait_sent(kind, m, source, target):
        def step(k, carry):
            exchange(kind, m, lax.rem(me + k, experts), me, source, target).wait_send()
            return carry

        lax.fori_loop(1, experts, step, 0)

    def wait_landed(kind, m, landed, source, target):
        exchange(kind, m, landed, landed, source, target).wait_recv()

    def save(index, m, source, target):
        return pltpu.make_async_copy(source, target.at[m], r.local.at[index, m])

    barrier = pltpu.get_barrier_semaphore()

    def greet(k, carry):
        pl.semaphore_signal(
            barrier, inc=1, device_id={"expert": lax.rem(me + k, experts)}, device_id_type=MESH
        )
        return carry

    lax.fori_loop(1, experts, greet, 0)
    pl.semaphore_signal(barrier, inc=1, device_id={"tensor": other}, device_id_type=MESH)

    @pl.when(sec > 0)
    def _():
        pl.semaphore_signal(barrier, inc=1, device_id={"section": sec - 1}, device_id_type=MESH)

    @pl.when(sec < sections - 1)
    def _():
        pl.semaphore_signal(barrier, inc=1, device_id={"section": sec + 1}, device_id_type=MESH)

    for m in range(micro):

        @pl.when(is_first)
        def _():
            save_in = pltpu.make_async_copy(r.inputs.at[m], r.x.at[m], r.local.at[0, m])
            save_in.start()

    weights = [
        pltpu.make_async_copy(source, target, r.fetch.at[k])
        for k, (source, target) in enumerate(
            ((r.gate, r.gate_v), (r.up, r.up_v), (r.down, r.down_v))
        )
    ]
    for copy in weights:
        copy.start()
    beside = (sec > 0).astype(i32) + (sec < sections - 1).astype(i32)
    pl.semaphore_wait(barrier, experts + beside)

    def seq_bias(m):
        row = iota((rows, 1), 0)
        start = jnp.zeros((rows, 1), i32)
        end = r.lengths[m, 0]
        for k in range(seqs):
            start = jnp.where(row >= end, row if k == seqs - 1 else end, start)
            end = end + r.lengths[m, min(k + 1, seqs)]
        for c in range(rows // chunk):
            piece = slice(c * chunk, (c + 1) * chunk)
            key = iota((chunk, rows), 1)
            seen = (key <= row[piece]) & (key >= start[piece])
            r.bias[piece, :] = jnp.where(seen, 0.0, -1e30)

    def routing(m):
        lane = iota((owned, LANES), 1)
        lane_t = iota((LANES, owned), 0)
        col = [r.route_col[m, :, k : k + 1] for k in range(2)]
        row = [r.route_row[m, k : k + 1, :] for k in range(2)]
        order_row, order_col = r.order_row[m], r.order_col[m]
        hot = [wide((lane == col[k]).astype(i32)) for k in range(2)]
        hot_t = [wide((lane_t == row[k]).astype(i32)) for k in range(2)]
        before = wide((order_row < order_col).astype(i32)).astype(bf16)
        before_t = wide((order_col < order_row).astype(i32)).astype(bf16)
        earlier = dot(before, (hot[0] + hot[1]).astype(bf16))
        earlier_t = dot((hot_t[0] + hot_t[1]).astype(bf16), before_t)
        for k in range(2):
            slot = jnp.sum(earlier * hot[k], axis=1, keepdims=True).astype(i32)
            slot_t = jnp.sum(earlier_t * hot_t[k], axis=0, keepdims=True).astype(i32)
            place = jnp.where((col[k] < experts) & (slot < cap), col[k] * cap_pad + slot, -1)
            place_t = jnp.where((row[k] < experts) & (slot_t < cap), row[k] * cap_pad + slot_t, -1)
            r.place_col[m, :, k : k + 1] = place
            r.place_row[m, k : k + 1, :] = place_t

    def spread(m, k):
        return flag(iota((owned, slots), 1) == r.place_col[m, :, k : k + 1]).astype(bf16)

    def spread_t(m, k):
        return flag(iota((slots, owned), 0) == r.place_row[m, k : k + 1, :]).astype(bf16)

    def choice_flags(m):
        col = [r.route_col[m, :, k : k + 1] for k in range(2)]
        copies = [wide((col[k] == experts + 1).astype(i32)) for k in range(2)]
        consts = [
            [wide((col[k] == experts + 2 + c).astype(i32)) for c in range(2)] for k in range(2)
        ]
        return col, copies, consts

    def unpack_gates(m):
        pack = r.gates[m]
        return [pack[:, k : k + 1] for k in range(2)], [pack[:, 2 + k : 3 + k] for k in range(2)]

    def through_expert(m, kind_in, kind_out, pair_in, pair_out, outgoing, arrived, target, kept, compute):
        mine = arrived.at[core]
        theirs = arrived.at[other]

        def arrive(j, carry):
            def one(k, inner):
                source = j * per_tile + k

                @pl.when(source != me)
                def _():
                    wait_landed(kind_in, m, source, outgoing, mine)

                return inner

            lax.fori_loop(0, per_tile, one, 0)
            pair(pair_in, m, j, mine.at[tile_of(j)], mine.at[tile_of(j)]).start()
            return carry

        lax.fori_loop(0, tiles, arrive, 0)
        passes = kind_in // 2

        def keep(half, tile, j):
            return pltpu.make_async_copy(
                arrived.at[half, tile], kept.at[m, half, tile], r.keep.at[passes, m, half, j]
            )

        def work(j, carry):
            tile = tile_of(j)
            keep(core, tile, j).start()
            r.partial[tile, :] = compute(core, tile, 0, j)
            pair(pair_in, m, j, theirs.at[tile], theirs.at[tile]).wait_recv()
            keep(other, tile, j).start()
            r.part_out[tile, :] = compute(other, tile, 1, j).astype(bf16)
            keep(other, tile, j).wait()
            pair(pair_out, m, j, r.part_out.at[tile], r.part_in.at[tile]).start()
            return carry

        lax.fori_loop(0, tiles, work, 0)

        def read(j, carry):
            tile = tile_of(j)
            pair(pair_in, m, j, mine.at[tile], mine.at[tile]).wait_send()
            keep(core, tile, j).wait()
            return carry

        lax.fori_loop(0, tiles, read, 0)

        def finish(j, carry):
            tile = tile_of(j)
            pair(pair_out, m, j, r.part_out.at[tile], r.part_in.at[tile]).wait_recv()
            r.result[tile, :] = (r.partial[tile, :] + wide(r.part_in[tile, :])).astype(bf16)

            def one(k, inner):
                source = j * per_tile + k

                @pl.when(source != me)
                def _():
                    exchange(kind_out, m, source, me, r.result, target).start()

                @pl.when(source == me)
                def _():
                    target[slot_rows(me), :] = r.result[slot_rows(me), :]

                return inner

            lax.fori_loop(0, per_tile, one, 0)
            return carry

        lax.fori_loop(0, tiles, finish, 0)

        def done(j, carry):
            tile = tile_of(j)
            pair(pair_out, m, j, r.part_out.at[tile], r.part_in.at[tile]).wait_send()
            return carry

        lax.fori_loop(0, tiles, done, 0)
        wait_sent(kind_in, m, outgoing, mine)

    def wait_back(m, kind_out, target):

        def one(k, carry):
            wait_landed(kind_out, m, lax.rem(me + k, experts), r.result, target)
            return carry

        lax.fori_loop(1, experts, one, 0)
        wait_sent(kind_out, m, r.result, target)

    def forward(m, carry):
        @pl.when(is_first)
        def _():
            pltpu.make_async_copy(r.inputs.at[m], r.x.at[m], r.local.at[0, m]).wait()

        @pl.when(sec > 0)
        def _():
            hop(0, m, r.hop_out, r.hop_in.at[0, m], sec - 1).wait_recv()
            r.x[m] = wide(r.hop_in[0, m])

        x = r.x[m]
        r.norm[m, own_rows, :] = (x * inverse_rms(x) * r.gain1[...]).astype(bf16)
        pair(P_NORM, m, 0, r.norm.at[m, own_rows], r.norm.at[m, own_rows]).start()
        routing(m)
        seq_bias(m)
        pair(P_NORM, m, 0, r.norm.at[m, other_rows], r.norm.at[m, other_rows]).wait_recv()
        save(1, m, r.norm.at[m], r.h_norm).start()

        normed = r.norm[m]
        for stash, weight in ((r.q, r.w_query), (r.k, r.w_key)):
            flat = dot(normed, weight[...])
            for p in range(pairs):
                lanes = slice(p * LANES, (p + 1) * LANES)
                stash[m, :, lanes] = turned(flat[:, lanes], r.cosine[...], r.sine[...]).astype(bf16)
        r.v[m] = dot(normed, r.w_value[...]).astype(bf16)

        r.logsum[m] = jnp.zeros((rows, LANES), f32)
        lane = iota((1, LANES), 1)

        def head_pair(p, inner):
            lanes = pl.ds(pl.multiple_of(p * LANES, LANES), LANES)
            q2, k2, v2 = r.q[m, :, lanes], r.k[m, :, lanes], r.v[m, :, lanes]
            for half in range(2):
                keep = wide(((lane // HEAD_DIM) == half).astype(i32)).astype(bf16)
                km, vm = k2 * keep, v2 * keep
                for c in range(rows // chunk):
                    piece, reach = slice(c * chunk, (c + 1) * chunk), (c + 1) * chunk
                    scores = dot_nt(q2[piece], km[:reach]) * scale + r.bias[piece, :reach]
                    peak = jnp.max(scores, axis=-1, keepdims=True)
                    shifted = jnp.exp(scores - peak)
                    total = jnp.sum(shifted, axis=-1, keepdims=True)
                    probs = (shifted * (1.0 / total)).astype(bf16)
                    mixed = dot(probs, vm[:reach])
                    if half == 0:
                        r.mix[piece, :] = mixed
                    else:
                        r.o[m, piece, lanes] = (r.mix[piece, :] + mixed).astype(bf16)
                    r.logsum[m, piece, :] = jnp.where(
                        lane == 2 * p + half, peak + jnp.log(total), r.logsum[m, piece, :]
                    )
            return inner

        lax.fori_loop(0, pairs, head_pair, 0)
        save(2, m, r.o.at[m], r.h_o).start()

        r.half_out[...] = dot(r.o[m, other_rows, :], r.w_out[...]).astype(bf16)
        pair(P_OUT, m, 0, r.half_out, r.half_in.at[0, m]).start()
        summed = x + dot(r.o[m, own_rows, :], r.w_out[...])
        pair(P_OUT, m, 0, r.half_out, r.half_in.at[0, m]).wait_recv()
        hidden = summed + wide(r.half_in[0, m])
        r.h[m] = hidden
        normed2 = (hidden * inverse_rms(hidden) * r.gain2[...]).astype(bf16)
        r.norm2[m] = normed2

        into = r.arrived
        both = spread_t(m, 0) + spread_t(m, 1)
        r.outgoing[...] = dot(both, normed2).astype(bf16)
        send_all(0, m, r.outgoing, into.at[core])
        r.arrived[core, slot_rows(me), :] = r.outgoing[slot_rows(me), :]

        mixer_hi, mixer_lo = halves(r.mixer[...])
        logits = dot_nt(normed2, mixer_hi) + dot_nt(normed2, mixer_lo)
        logits = logits + dot3(dot, r.prev[m], r.residual[...])
        col, copies, consts = choice_flags(m)
        wide_lane = iota((owned, LANES), 1)
        picked = [
            jnp.sum(jnp.where(wide_lane == col[k], logits, 0.0), axis=1, keepdims=True)
            for k in range(2)
        ]
        gate = [jax.nn.sigmoid(picked[0] - picked[1]), jax.nn.sigmoid(picked[1] - picked[0])]
        rate = [jax.nn.sigmoid(logits[:, choices + c : choices + c + 1]) for c in range(2)]
        pack = jnp.zeros((owned, LANES), f32)
        for k, value in enumerate(gate + rate):
            pack = jnp.where(wide_lane == k, value, pack)
        r.gates[m] = pack

        @pl.when(m == 0)
        def _():
            for copy in weights:
                copy.wait()

        def compute(half, tile, slot, j):
            block = r.arrived[half, tile, :]
            place = pl.ds(pl.multiple_of(half * slots + tile.start, tile_rows), tile_rows)
            value = dot(block, r.gate_v[...])
            upper = dot(block, r.up_v[...])
            sig = jax.nn.sigmoid(value)
            active = value * sig
            inside = (active * upper).astype(bf16)
            r.by_up[place, :] = active.astype(bf16)
            r.by_gate[place, :] = (upper * sig * (1.0 + value * (1.0 - sig))).astype(bf16)

            def ring(at):
                rows_of = pl.ds(pl.multiple_of(half * slots + at * tile_rows, tile_rows), tile_rows)
                return pltpu.make_async_copy(
                    r.inside.at[slot], r.h_inside.at[m, rows_of], r.ring.at[slot, m, at]
                )

            @pl.when(j > 0)
            def _():
                ring(j - 1).wait()

            r.inside[slot] = inside
            ring(j).start()

            @pl.when(j == tiles - 1)
            def _():
                ring(j).wait()

            return dot(inside, r.down_v[...])

        through_expert(m, 0, 1, P_ROWS, P_PART, r.outgoing, into, r.back.at[m], r.h_rows, compute)
        stored = [
            save(5, m, r.by_up, r.h_up),
            save(6, m, r.by_gate, r.h_gate),
        ]
        for copy in stored:
            copy.start()
        wait_back(m, 1, r.back.at[m])

        apart = [dot(spread(m, k), r.back[m]) for k in range(2)]
        out = r.h[m] + gate[0] * apart[0] + gate[1] * apart[1]
        own = gate[0] * copies[0] + gate[1] * copies[1]
        for c in range(2):
            on = gate[0] * consts[0][c] + gate[1] * consts[1][c]
            own = own + on * rate[c]
            out = out + (on * (1.0 - rate[c])) * r.const_value[c : c + 1, :]
        out = out + own * wide(r.norm2[m])
        r.stage[...] = out
        save(3, m, r.stage, r.layer_out).start()

        @pl.when(sec < sections - 1)
        def _():
            copy = hop(0, m, r.hop_out, r.hop_in.at[0, m], sec + 1)
            r.hop_out[...] = out.astype(bf16)
            copy.start()
            copy.wait_send()

        pair(P_NORM, m, 0, r.norm.at[m, own_rows], r.norm.at[m, own_rows]).wait_send()
        pair(P_OUT, m, 0, r.half_out, r.half_in.at[0, m]).wait_send()
        save(3, m, r.stage, r.layer_out).wait()
        save(1, m, r.norm.at[m], r.h_norm).wait()
        save(2, m, r.o.at[m], r.h_o).wait()
        for copy in stored:
            copy.wait()
        return carry

    lax.fori_loop(0, micro, forward, 0)

    r.mixer_grad[...] = jnp.zeros_like(r.mixer_grad)
    r.residual_grad[...] = jnp.zeros_like(r.residual_grad)
    r.rows_grad[...] = jnp.zeros_like(r.rows_grad)

    def backward(m, carry):
        fetched = [
            pltpu.make_async_copy(r.h_up.at[m], r.by_up, r.local.at[7, m]),
            pltpu.make_async_copy(r.h_gate.at[m], r.by_gate, r.local.at[8, m]),
        ]
        for copy in fetched:
            copy.start()

        @pl.when(is_last)
        def _():
            copy = pltpu.make_async_copy(r.cotangent.at[m], r.dz, r.local.at[9, m])
            copy.start()
            copy.wait()

        @pl.when(sec < sections - 1)
        def _():
            hop(1, m, r.hop_out, r.hop_in.at[1, m], sec + 1).wait_recv()
            r.dz[...] = wide(r.hop_in[1, m])

        dz = r.dz[...]
        gate, rate = unpack_gates(m)
        into = r.arrived
        leaving = [dot(spread_t(m, k), (gate[k] * dz).astype(bf16)) for k in range(2)]
        r.outgoing[...] = (leaving[0] + leaving[1]).astype(bf16)
        send_all(2, m, r.outgoing, into.at[core])
        r.arrived[core, slot_rows(me), :] = r.outgoing[slot_rows(me), :]

        col, copies, consts = choice_flags(m)
        normed2 = r.norm2[m]
        dz_norm = jnp.sum(dz * wide(normed2), axis=1, keepdims=True)
        dz_const = [
            jnp.sum(dz * r.const_value[c : c + 1, :], axis=1, keepdims=True) for c in range(2)
        ]
        apart = [dot(spread(m, k), r.back[m]) for k in range(2)]
        dgate = []
        for k in range(2):
            value = jnp.sum(dz * apart[k], axis=1, keepdims=True)
            value = value + copies[k] * dz_norm
            for c in range(2):
                value = value + consts[k][c] * (rate[c] * dz_norm + (1.0 - rate[c]) * dz_const[c])
            dgate.append(value)
        coupled = gate[0] * gate[1] * (dgate[0] - dgate[1])
        lane = iota((owned, LANES), 1)
        dlogits = jnp.where(lane == col[0], coupled, jnp.where(lane == col[1], -coupled, 0.0))
        own = gate[0] * copies[0] + gate[1] * copies[1]
        for c in range(2):
            on = gate[0] * consts[0][c] + gate[1] * consts[1][c]
            own = own + on * rate[c]
            dmix = on * (dz_norm - dz_const[c]) * rate[c] * (1.0 - rate[c])
            dlogits = dlogits + jnp.where(lane == choices + c, dmix, 0.0)
            r.rows_grad[c : c + 1, :] += jnp.sum((on * (1.0 - rate[c])) * dz, axis=0, keepdims=True)
        dlogits_hi, dlogits_lo = halves(dlogits)
        r.mixer_grad[...] += dot_tn(dlogits_hi, normed2) + dot_tn(dlogits_lo, normed2)
        r.residual_grad[...] += dot3(dot_tn, r.prev[m], dlogits)
        r.logit_grad[m] = dot3(dot_nt, dlogits, r.residual[...])
        r.dnorm[...] = dot3(dot, dlogits, r.mixer[...]) + own * dz
        seq_bias(m)
        for copy in fetched:
            copy.wait()

        def compute(half, tile, slot, j):
            block = r.arrived[half, tile, :]
            place = pl.ds(pl.multiple_of(half * slots + tile.start, tile_rows), tile_rows)
            dinside = dot_nt(block, r.down_v[...])
            dvalue = (dinside * wide(r.by_gate[place, :])).astype(bf16)
            dupper = (dinside * wide(r.by_up[place, :])).astype(bf16)
            r.by_gate[place, :] = dvalue
            r.by_up[place, :] = dupper
            return dot_nt(dvalue, r.gate_v[...]) + dot_nt(dupper, r.up_v[...])

        through_expert(m, 2, 3, P_GROWS, P_GPART, r.outgoing, into, r.grad_back, r.h_grads, compute)
        stored = [
            save(11, m, r.by_up, r.h_up),
            save(12, m, r.by_gate, r.h_gate),
        ]
        for copy in stored:
            copy.start()
        wait_back(m, 3, r.grad_back)

        both = spread(m, 0) + spread(m, 1)
        dnorm = r.dnorm[...] + dot(both, r.grad_back[...])
        hidden = r.h[m]
        root = inverse_rms(hidden)
        scaled = dnorm * r.gain2[...]
        pull = root * root * root * jnp.mean(hidden * scaled, axis=-1, keepdims=True)
        dhidden = dz + root * scaled - hidden * pull
        r.rows_grad[3:4, :] += jnp.sum(dnorm * hidden * root, axis=0, keepdims=True)
        r.dh[...] = dhidden
        r.da[own_rows, :] = dhidden.astype(bf16)
        pair(P_DA, m, 0, r.da.at[own_rows], r.da.at[own_rows]).start()
        pair(P_DA, m, 0, r.da.at[other_rows], r.da.at[other_rows]).wait_recv()
        save_da = save(13, m, r.da, r.h_da)
        save_da.start()
        r.do[...] = dot_nt(r.da[...], r.w_out[...]).astype(bf16)

        head_lane = iota((1, LANES), 1)

        def head_pair(p, inner):
            lanes = pl.ds(pl.multiple_of(p * LANES, LANES), LANES)
            q2, k2, v2 = r.q[m, :, lanes], r.k[m, :, lanes], r.v[m, :, lanes]
            do2 = r.do[:, lanes]
            for half in range(2):
                keep = wide(((head_lane // HEAD_DIM) == half).astype(i32)).astype(bf16)
                km, vm, qm, dom = k2 * keep, v2 * keep, q2 * keep, do2 * keep
                for c in range(rows // chunk):
                    piece, reach = slice(c * chunk, (c + 1) * chunk), (c + 1) * chunk
                    scores = dot_nt(q2[piece], km[:reach]) * scale + r.bias[piece, :reach]
                    total = jnp.sum(
                        jnp.where(head_lane == 2 * p + half, r.logsum[m, piece, :], 0.0),
                        axis=1,
                        keepdims=True,
                    )
                    probs = jnp.exp(scores - total)
                    dprobs = dot_nt(do2[piece], vm[:reach])
                    meant = jnp.sum(dprobs * probs, axis=-1, keepdims=True)
                    dscores = (probs * (dprobs - meant)).astype(bf16)
                    dq = dot(dscores, km[:reach])
                    dk = dot_tn(dscores, qm[piece])
                    dv = dot_tn(probs.astype(bf16), dom[piece])
                    if half == 0:
                        r.mix[piece, :] = dq
                    else:
                        r.mix[piece, :] += dq
                    if half == 0 and c == 0:
                        r.mix_k[...] = jnp.zeros_like(r.mix_k)
                        r.mix_v[...] = jnp.zeros_like(r.mix_v)
                    r.mix_k[:reach, :] += dk
                    r.mix_v[:reach, :] += dv
            r.dq[:, lanes] = (turned_back(r.mix[...], r.cosine[...], r.sine[...]) * scale).astype(bf16)
            r.dk[:, lanes] = (turned_back(r.mix_k[...], r.cosine[...], r.sine[...]) * scale).astype(bf16)
            r.dv[:, lanes] = r.mix_v[...].astype(bf16)
            return inner

        lax.fori_loop(0, pairs, head_pair, 0)
        more = [save(14, m, r.dq, r.h_dq), save(15, m, r.dk, r.h_dk), save(16, m, r.dv, r.h_dv)]
        for copy in more:
            copy.start()

        def dnormed(piece):
            return (
                dot_nt(r.dq[piece, :], r.w_query[...])
                + dot_nt(r.dk[piece, :], r.w_key[...])
                + dot_nt(r.dv[piece, :], r.w_value[...])
            )

        r.half_out[...] = dnormed(other_rows).astype(bf16)
        pair(P_DX, m, 0, r.half_out, r.half_in.at[1, m]).start()
        kept = dnormed(own_rows)
        pair(P_DX, m, 0, r.half_out, r.half_in.at[1, m]).wait_recv()
        dnorm1 = kept + wide(r.half_in[1, m])
        x = r.x[m]
        root1 = inverse_rms(x)
        scaled1 = dnorm1 * r.gain1[...]
        pull1 = root1 * root1 * root1 * jnp.mean(x * scaled1, axis=-1, keepdims=True)
        dx = r.dh[...] + root1 * scaled1 - x * pull1
        r.stage[...] = dx
        save(4, m, r.stage, r.input_grad).start()

        @pl.when(sec > 0)
        def _():
            copy = hop(1, m, r.hop_out, r.hop_in.at[1, m], sec - 1)
            r.hop_out[...] = dx.astype(bf16)
            copy.start()
            copy.wait_send()

        r.rows_grad[2:3, :] += jnp.sum(dnorm1 * x * root1, axis=0, keepdims=True)
        pair(P_DA, m, 0, r.da.at[own_rows], r.da.at[own_rows]).wait_send()
        pair(P_DX, m, 0, r.half_out, r.half_in.at[1, m]).wait_send()
        save(4, m, r.stage, r.input_grad).wait()
        save_da.wait()
        for copy in stored + more:
            copy.wait()
        return carry

    lax.fori_loop(0, micro, backward, 0)


def run_chain(cfg, ins):
    vmem, anywhere = pl.BlockSpec(memory_space=pltpu.VMEM), pl.BlockSpec(memory_space=pl.ANY)
    smem = pl.BlockSpec(memory_space=pltpu.SMEM)
    far = {"inputs", "cotangent", "gate", "up", "down"}
    micro, owned, rows, width, inner = cfg.micro, cfg.owned, cfg.rows, cfg.width, cfg.inner
    heads_width, slots = cfg.heads * HEAD_DIM, cfg.slots
    shape = jax.ShapeDtypeStruct
    outs = dict(
        logit_grad=shape((micro, owned, LANES), f32),
        mixer_grad=shape((LANES, width), f32),
        residual_grad=shape((LANES, LANES), f32),
        rows_grad=shape((8, width), f32),
    )
    hbm_outs = dict(
        layer_out=shape((micro, owned, width), f32),
        input_grad=shape((micro, owned, width), f32),
        h_rows=shape((micro, 2, slots, width), bf16),
        h_grads=shape((micro, 2, slots, width), bf16),
        h_inside=shape((micro, 2 * slots, inner), bf16),
        h_up=shape((micro, 2 * slots, inner), bf16),
        h_gate=shape((micro, 2 * slots, inner), bf16),
        h_norm=shape((micro, rows, width), bf16),
        h_da=shape((micro, rows, width), bf16),
        h_o=shape((micro, rows, heads_width), bf16),
        h_dq=shape((micro, rows, heads_width), bf16),
        h_dk=shape((micro, rows, heads_width), bf16),
        h_dv=shape((micro, rows, heads_width), bf16),
    )
    dma = pltpu.SemaphoreType.DMA
    scratch = dict(
        gate_v=pltpu.VMEM((width, inner), bf16),
        up_v=pltpu.VMEM((width, inner), bf16),
        down_v=pltpu.VMEM((inner, width), bf16),
        x=pltpu.VMEM((micro, owned, width), f32),
        h=pltpu.VMEM((micro, owned, width), f32),
        norm=pltpu.VMEM((micro, rows, width), bf16),
        norm2=pltpu.VMEM((micro, owned, width), bf16),
        q=pltpu.VMEM((micro, rows, heads_width), bf16),
        k=pltpu.VMEM((micro, rows, heads_width), bf16),
        v=pltpu.VMEM((micro, rows, heads_width), bf16),
        o=pltpu.VMEM((micro, rows, heads_width), bf16),
        logsum=pltpu.VMEM((micro, rows, LANES), f32),
        gates=pltpu.VMEM((micro, owned, LANES), f32),
        place_col=pltpu.VMEM((micro, owned, 2), i32),
        place_row=pltpu.VMEM((micro, 2, owned), i32),
        bias=pltpu.VMEM((rows, rows), f32),
        arrived=pltpu.VMEM((2, slots, width), bf16),
        part_in=pltpu.VMEM((slots, width), bf16),
        back=pltpu.VMEM((micro, slots, width), bf16),
        half_in=pltpu.VMEM((2, micro, owned, width), bf16),
        hop_in=pltpu.VMEM((2, micro, owned, width), bf16),
        grad_back=pltpu.VMEM((slots, width), bf16),
        outgoing=pltpu.VMEM((slots, width), bf16),
        part_out=pltpu.VMEM((slots, width), bf16),
        result=pltpu.VMEM((slots, width), bf16),
        partial=pltpu.VMEM((slots, width), f32),
        half_out=pltpu.VMEM((owned, width), bf16),
        hop_out=pltpu.VMEM((owned, width), bf16),
        inside=pltpu.VMEM((2, cfg.tile_rows, inner), bf16),
        by_up=pltpu.VMEM((2 * slots, inner), bf16),
        by_gate=pltpu.VMEM((2 * slots, inner), bf16),
        dz=pltpu.VMEM((owned, width), f32),
        stage=pltpu.VMEM((owned, width), f32),
        dh=pltpu.VMEM((owned, width), f32),
        dnorm=pltpu.VMEM((owned, width), f32),
        da=pltpu.VMEM((rows, width), bf16),
        do=pltpu.VMEM((rows, heads_width), bf16),
        dq=pltpu.VMEM((rows, heads_width), bf16),
        dk=pltpu.VMEM((rows, heads_width), bf16),
        dv=pltpu.VMEM((rows, heads_width), bf16),
        mix=pltpu.VMEM((rows, LANES), f32),
        mix_k=pltpu.VMEM((rows, LANES), f32),
        mix_v=pltpu.VMEM((rows, LANES), f32),
        pair_send=dma((8, micro, cfg.tiles)),
        pair_recv=dma((8, micro, cfg.tiles)),
        hop_send=dma((2, micro)),
        hop_recv=dma((2, micro)),
        a2a_send=dma((4, micro, cfg.experts)),
        a2a_recv=dma((4, micro, cfg.experts)),
        local=dma((17, micro)),
        keep=dma((2, micro, 2, cfg.tiles)),
        ring=dma((2, micro, cfg.tiles)),
        fetch=dma((3,)),
    )
    names = [*ins, *outs, *hbm_outs, *scratch]
    flops = 2 * micro * (2 * slots * width * inner * 6 + rows * width * heads_width * 10)
    results = pl.pallas_call(
        functools.partial(chain_kernel, cfg, names),
        out_shape=[*outs.values(), *hbm_outs.values()],
        in_specs=[
            smem if name == "lengths" else anywhere if name in far else vmem for name in ins
        ],
        out_specs=[vmem] * len(outs) + [anywhere] * len(hbm_outs),
        scratch_shapes=[*scratch.values()],
        compiler_params=pltpu.CompilerParams(
            collective_id=0, has_side_effects=True, vmem_limit_bytes=60 * 2**20
        ),
        cost_estimate=pl.CostEstimate(flops=flops, bytes_accessed=50_000_000, transcendentals=0),
    )(*ins.values())
    return types.SimpleNamespace(**dict(zip([*outs, *hbm_outs], results, strict=True)))


def tail_kernel(cfg, names, *refs):
    r = types.SimpleNamespace(**dict(zip(names, refs, strict=True)))
    experts, width, pad = cfg.experts, cfg.width, cfg.small_pad
    side = width // 2
    outer = experts // 2
    me, core = lax.axis_index("expert"), lax.axis_index("tensor")
    mine_out, mine_in = me // 2, lax.rem(me, 2)
    beside = me + 1 - 2 * mine_in
    pieces = len(cfg.piece_rows)
    starts = [sum(cfg.piece_rows[:c]) * experts for c in range(pieces)]

    def peer_of(k):
        place = lax.rem(mine_out + k, outer)
        return place, place * 2 + mine_in

    barrier = pltpu.get_barrier_semaphore()
    pl.semaphore_signal(barrier, inc=1, device_id={"tensor": 1 - core}, device_id_type=MESH)
    pl.semaphore_signal(barrier, inc=1, device_id={"expert": beside}, device_id_type=MESH)

    def greet(k, carry):
        pl.semaphore_signal(barrier, inc=1, device_id={"expert": peer_of(k)[1]}, device_id_type=MESH)
        return carry

    lax.fori_loop(1, outer, greet, 0)

    loads = [
        pltpu.make_async_copy(source, target, r.fetch.at[k])
        for k, (source, target) in enumerate(
            (
                (r.h_rows, r.rows_v),
                (r.h_gate, r.gate_v),
                (r.h_up, r.up_v),
                (r.h_grads, r.grads_v),
                (r.h_inside, r.gate_v),
            )
        )
    ]
    for copy in loads[:4]:
        copy.start()

    r.pack[...] = jnp.zeros_like(r.pack)
    r.pack[:pad, :] = r.mixer_grad[:pad, :side]
    r.pack[pad : 2 * pad, :] = r.mixer_grad[:pad, side:]
    r.pack[2 * pad : 2 * pad + 8, :] = r.rows_grad[:, :side]
    r.pack[2 * pad + 8 : 2 * pad + 16, :] = r.rows_grad[:, side:]
    r.pack[2 * pad + 16 : 3 * pad + 16, :LANES] = r.residual_grad[:pad, :]
    r.pack_out[...] = r.pack[...].astype(bf16)
    pl.semaphore_wait(barrier, outer + 1)
    pack_copy = pltpu.make_async_remote_copy(
        src_ref=r.pack_out,
        dst_ref=r.pack_in,
        send_sem=r.pack_sem.at[0],
        recv_sem=r.pack_sem.at[1],
        device_id={"tensor": 1 - core},
        device_id_type=MESH,
    )
    pack_copy.start()

    def span(start, index, size):
        return pl.ds(pl.multiple_of(start + index * size, 16), size)

    def over_x(stage, c, source, target, from_rows, to_rows):
        return pltpu.make_async_remote_copy(
            src_ref=source.at[from_rows],
            dst_ref=target.at[to_rows],
            send_sem=r.x_send.at[stage, c],
            recv_sem=r.x_recv.at[stage, c],
            device_id={"expert": beside},
            device_id_type=MESH,
        )

    def over_z(stage, c, place, landed, peer, source, target):
        return pltpu.make_async_remote_copy(
            src_ref=source,
            dst_ref=target,
            send_sem=r.z_send.at[stage, c, place],
            recv_sem=r.z_recv.at[stage, c, landed],
            device_id={"expert": peer},
            device_id_type=MESH,
        )

    def half_of(c, which):
        return span(starts[c], which, outer * cfg.piece_rows[c])

    def landing(c):
        return pl.ds(starts[c] // 2, outer * cfg.piece_rows[c])

    def scatter_x(c):
        return over_x(0, c, r.sent, r.x_in, half_of(c, 1 - mine_in), landing(c))

    def gather_x(c, which):
        return over_x(1, c, r.summed, r.summed, half_of(c, which), half_of(c, which))

    def scatter_z(c, place, landed, peer):
        size = cfg.piece_rows[c]
        return over_z(
            0,
            c,
            place,
            landed,
            peer,
            r.z_out.at[span(starts[c] // 2, place, size)],
            r.z_in.at[landed, pl.ds(starts[c] // experts, size)],
        )

    def final(c, place):
        return span(starts[c], mine_in * outer + place, cfg.piece_rows[c])

    def gather_z(c, place, landed, peer):
        rows = final(c, landed)
        return over_z(1, c, place, landed, peer, r.summed.at[rows], r.summed.at[rows])

    def weight_grad(left, right):
        return dot_tn(left.reshape(-1, left.shape[-1]), right.reshape(-1, right.shape[-1]))

    products = ((r.h_norm, r.h_dq), (r.h_norm, r.h_dk), (r.h_norm, r.h_dv), (r.h_da, r.h_o))
    for c in range(pieces):
        rows = pl.ds(starts[c], experts * cfg.piece_rows[c])
        if c < 4:
            left, right = products[c]
            value = weight_grad(left[...], right[...])
            if value.shape[0] != experts * cfg.piece_rows[c]:
                r.sent[rows, :] = jnp.zeros((experts * cfg.piece_rows[c], side), bf16)
            r.sent[pl.ds(starts[c], value.shape[0]), :] = value.astype(bf16)
        else:
            pack_copy.wait()
            r.sent[rows, :] = (r.pack[...] + wide(r.pack_in[...])).astype(bf16)
        scatter_x(c).start()

    rows_all = cfg.micro * 2 * cfg.slots
    tile = 256
    steps = []
    for left, right, target in (
        (r.rows_v, r.gate_v, r.gate_grad),
        (r.rows_v, r.up_v, r.up_grad),
        (r.gate_v, r.grads_v, r.down_grad),
    ):
        for t in range(left.shape[-1] // tile):
            needs = ((0, 1), (0, 2), (3, 4))[len(steps) // (width // tile) if target is not r.down_grad else 2]
            steps.append((left, right, target, t, needs))

    loaded = set()
    flying = [None, None]

    def expert_step(index):
        left, right, target, t, needs = steps[index]
        if index == width // tile:
            loads[4].start()
        for k in needs:
            if k not in loaded:
                loads[k].wait()
                loaded.add(k)
        slot = index % 2
        if flying[slot] is not None:
            flying[slot].wait()
        wide_out = right.shape[-1]
        a = left[..., t * tile : (t + 1) * tile].reshape(rows_all, tile)
        r.stage[slot, :, :wide_out] = dot_tn(a, right[...].reshape(rows_all, wide_out))
        copy = pltpu.make_async_copy(
            r.stage.at[slot, :, pl.ds(0, wide_out)],
            target.at[pl.ds(t * tile, tile)],
            r.step_sem.at[index],
        )
        copy.start()
        flying[slot] = copy

    done = 0
    for c in range(pieces):
        upto = len(steps) * (c + 1) // pieces
        while done < upto:
            expert_step(done)
            done += 1
        scatter_x(c).wait_recv()
        rows = landing(c)
        r.z_out[rows, :] = (wide(r.sent[half_of(c, mine_in), :]) + wide(r.x_in[rows, :])).astype(bf16)

        def out_z(k, carry, c=c):
            place, peer = peer_of(k)
            scatter_z(c, place, mine_out, peer).start()
            return carry

        lax.fori_loop(1, outer, out_z, 0)

    for c in range(pieces):
        size = cfg.piece_rows[c]

        def add_z(k, total, c=c, size=size):
            place, peer = peer_of(k)
            scatter_z(c, place, place, peer).wait_recv()
            return total + wide(r.z_in[place, pl.ds(starts[c] // experts, size), :])

        total = lax.fori_loop(1, outer, add_z, wide(r.z_out[span(starts[c] // 2, mine_out, size), :]))
        r.summed[final(c, mine_out), :] = total.astype(bf16)

        def back_z(k, carry, c=c):
            place, peer = peer_of(k)
            gather_z(c, place, mine_out, peer).start()
            return carry

        lax.fori_loop(1, outer, back_z, 0)

    for c in range(pieces):

        def wait_z(k, carry, c=c):
            place, peer = peer_of(k)
            gather_z(c, place, place, peer).wait_recv()
            return carry

        lax.fori_loop(1, outer, wait_z, 0)
        gather_x(c, mine_in).start()
    for c in range(pieces):
        gather_x(c, 1 - mine_in).wait_recv()
    for c in range(pieces):
        scatter_x(c).wait_send()
        gather_x(c, mine_in).wait_send()

        def sent_z(k, carry, c=c):
            place, peer = peer_of(k)
            scatter_z(c, place, mine_out, peer).wait_send()
            gather_z(c, place, mine_out, peer).wait_send()
            return carry

        lax.fori_loop(1, outer, sent_z, 0)
    for copy in flying:
        copy.wait()


def run_tail(cfg, got):
    vmem, anywhere = pl.BlockSpec(memory_space=pltpu.VMEM), pl.BlockSpec(memory_space=pl.ANY)
    micro, width, inner, slots, experts = cfg.micro, cfg.width, cfg.inner, cfg.slots, cfg.experts
    side, outer = width // 2, experts // 2
    piece = -(-width // (16 * experts)) * 16
    small = -(-(3 * cfg.small_pad + 16) // (16 * experts)) * 16
    cfg.piece_rows = [piece] * 4 + [small]
    total = sum(cfg.piece_rows) * experts
    near = dict(
        h_norm=got.h_norm,
        h_da=got.h_da,
        h_o=got.h_o,
        h_dq=got.h_dq,
        h_dk=got.h_dk,
        h_dv=got.h_dv,
        mixer_grad=got.mixer_grad,
        residual_grad=got.residual_grad,
        rows_grad=got.rows_grad,
    )
    far = dict(
        h_rows=got.h_rows,
        h_grads=got.h_grads,
        h_inside=got.h_inside,
        h_up=got.h_up,
        h_gate=got.h_gate,
    )
    shape, dma = jax.ShapeDtypeStruct, pltpu.SemaphoreType.DMA
    outs = dict(
        summed=shape((total, side), bf16),
        gate_grad=shape((width, inner), f32),
        up_grad=shape((width, inner), f32),
        down_grad=shape((inner, width), f32),
    )
    scratch = dict(
        rows_v=pltpu.VMEM((micro, 2, slots, width), bf16),
        grads_v=pltpu.VMEM((micro, 2, slots, width), bf16),
        up_v=pltpu.VMEM((micro, 2 * slots, inner), bf16),
        gate_v=pltpu.VMEM((micro, 2 * slots, inner), bf16),
        sent=pltpu.VMEM((total, side), bf16),
        x_in=pltpu.VMEM((total // 2, side), bf16),
        z_out=pltpu.VMEM((total // 2, side), bf16),
        z_in=pltpu.VMEM((outer, total // experts, side), bf16),
        pack=pltpu.VMEM((small * experts, side), f32),
        pack_out=pltpu.VMEM((small * experts, side), bf16),
        pack_in=pltpu.VMEM((small * experts, side), bf16),
        stage=pltpu.VMEM((2, 256, max(inner, width)), f32),
        fetch=dma((5,)),
        step_sem=dma(((2 * width + inner) // 256,)),
        pack_sem=dma((2,)),
        x_send=dma((2, 5)),
        x_recv=dma((2, 5)),
        z_send=dma((2, 5, outer)),
        z_recv=dma((2, 5, outer)),
    )
    names = [*near, *far, *outs, *scratch]
    results = pl.pallas_call(
        functools.partial(tail_kernel, cfg, names),
        out_shape=[*outs.values()],
        in_specs=[vmem] * len(near) + [anywhere] * len(far),
        out_specs=[vmem] + [anywhere] * 3,
        scratch_shapes=[*scratch.values()],
        compiler_params=pltpu.CompilerParams(
            collective_id=1, has_side_effects=True, vmem_limit_bytes=60 * 2**20
        ),
        cost_estimate=pl.CostEstimate(
            flops=12 * micro * slots * width * inner, bytes_accessed=40_000_000, transcendentals=0
        ),
    )(*near.values(), *far.values())
    return types.SimpleNamespace(
        **dict(zip(outs, results, strict=True)), pad_rows=piece * experts
    )


def rope_tables(rows):
    half_width = HEAD_DIM // 2
    frequency = 10000.0 ** (-2.0 * np.arange(half_width, dtype=np.float64) / HEAD_DIM)
    angles = np.arange(rows, dtype=np.float64)[:, None] * frequency[None, :]
    angles = np.tile(angles, (1, LANES // half_width))
    return np.cos(angles).astype(np.float32), np.sin(angles).astype(np.float32)


def local(
    inputs,
    cotangent,
    prev_logits,
    lengths,
    routes,
    slot_order,
    norm_gain1,
    w_query,
    w_key,
    w_value,
    w_out,
    norm_gain2,
    router,
    router_residual,
    const_gate,
    const_value,
    expert_gate,
    expert_up,
    expert_down,
):
    micro, owned, width = inputs.shape
    tensors, peers = lax.axis_size("tensor"), lax.axis_size("expert")
    choices = router.shape[2]
    experts = choices - 4
    assert experts == peers and tensors == 2
    cap = 9 * 2 * owned // (8 * choices) + 1
    cap_pad = -(-cap // 16) * 16
    per_tile = max(d for d in range(1, peers + 1) if peers % d == 0 and d * cap_pad <= 256)
    cfg = types.SimpleNamespace(
        micro=micro,
        owned=owned,
        width=width,
        rows=owned * tensors,
        inner=expert_gate.shape[3],
        heads=w_query.shape[2] // HEAD_DIM,
        experts=experts,
        choices=choices,
        cap=cap,
        cap_pad=cap_pad,
        slots=peers * cap_pad,
        per_tile=per_tile,
        tiles=peers // per_tile,
        tile_rows=per_tile * cap_pad,
        sections=lax.axis_size("section"),
        seqs=lengths.shape[2] - 1,
        chunk=owned,
        small_pad=-(-(choices + 2) // 16) * 16,
    )
    cosine, sine = rope_tables(cfg.rows)
    mixer = jnp.concatenate(
        [router[0].T, const_gate[0], jnp.zeros((LANES - choices - 2, width), f32)], axis=0
    )
    lane_pad = LANES - choices
    ins = dict(
        lengths=lengths[:, 0],
        inputs=inputs,
        cotangent=cotangent,
        prev=jnp.pad(prev_logits[0], ((0, 0), (0, 0), (0, lane_pad))),
        route_col=routes[0],
        route_row=jnp.swapaxes(routes[0], 1, 2),
        order_row=slot_order[0],
        order_col=jnp.swapaxes(slot_order[0], 1, 2),
        gain1=norm_gain1,
        gain2=norm_gain2,
        w_query=w_query[0],
        w_key=w_key[0],
        w_value=w_value[0],
        w_out=w_out[0],
        mixer=mixer,
        residual=jnp.pad(router_residual[0], ((0, lane_pad), (0, lane_pad))),
        const_value=const_value[0],
        cosine=jnp.asarray(cosine),
        sine=jnp.asarray(sine),
        gate=expert_gate[0, 0],
        up=expert_up[0, 0],
        down=expert_down[0, 0],
    )
    got = run_chain(cfg, ins)

    tail = run_tail(cfg, got)
    query_grad, key_grad, value_grad, out_grad = (
        wide(tail.summed[c * tail.pad_rows : c * tail.pad_rows + width]) for c in range(4)
    )
    small = wide(tail.summed[4 * tail.pad_rows :])
    pad = cfg.small_pad
    mixer_grad = jnp.concatenate([small[:pad], small[pad : 2 * pad]], axis=1)
    rows_grad = jnp.concatenate([small[2 * pad : 2 * pad + 8], small[2 * pad + 8 : 2 * pad + 16]], axis=1)
    residual_grad = small[2 * pad + 16 : 3 * pad + 16, :LANES]
    return (
        got.layer_out[None],
        got.input_grad[None],
        got.logit_grad[None, :, :, :choices],
        rows_grad[None, 2],
        query_grad[None],
        key_grad[None],
        value_grad[None],
        out_grad.T[None],
        rows_grad[None, 3],
        mixer_grad[:choices].T[None],
        residual_grad[None, :choices, :choices],
        mixer_grad[None, choices : choices + 2],
        rows_grad[None, :2],
        tail.gate_grad[None, None],
        tail.up_grad[None, None],
        tail.down_grad[None, None],
    )


def solution(mesh):
    tokens = ("expert", "tensor")
    in_specs = (
        P(None, tokens, None),
        P(None, tokens, None),
        P("section", None, tokens, None),
        P(None, "expert", None),
        P("section", None, tokens, None),
        P("section", None, tokens, None),
        P("section", None),
        P("section", None, "tensor"),
        P("section", None, "tensor"),
        P("section", None, "tensor"),
        P("section", "tensor", None),
        P("section", None),
        P("section", None, None),
        P("section", None, None),
        P("section", None, None),
        P("section", None, None),
        P("section", "expert", None, "tensor"),
        P("section", "expert", None, "tensor"),
        P("section", "expert", "tensor", None),
    )
    out_specs = (
        P("section", None, tokens, None),
        P("section", None, tokens, None),
        P("section", None, tokens, None),
        P("section", None),
        P("section", None, "tensor"),
        P("section", None, "tensor"),
        P("section", None, "tensor"),
        P("section", "tensor", None),
        P("section", None),
        P("section", None, None),
        P("section", None, None),
        P("section", None, None),
        P("section", None, None),
        P("section", "expert", None, "tensor"),
        P("section", "expert", None, "tensor"),
        P("section", "expert", "tensor", None),
    )
    return jax.shard_map(local, mesh=mesh, in_specs=in_specs, out_specs=out_specs, check_vma=False)
```

time: 1170 us -> 509 us (0.44); the launches traced: 1150 us -> 509 us
  Pallas kernels: 0 us -> 477 us
  matrix products: 271 us -> 0 us
  local copies, waits for them, and re-layouts: 275 us -> 22.9 us
  other arithmetic: 216 us -> 7.79 us
  waiting for transfers between devices: 191 us -> 0 us
  blocking collectives: 93.7 us -> 0 us
  starting transfers between devices: 82.6 us -> 0 us
  between operations: 19.4 us -> 0.71 us
    pallas_call x0 -> x2, Pallas kernels: none -> 477 us  [the longest x1 391 us: run_chain(): pl.pallas_call(functools.partial(chain_kernel, cfg, names), out_shape=[*o...]
    dot_general x120 -> x0, matrix products: 271 us -> none  [the longest x27 76.1 us: dot_plain(): return jnp.dot(left, right, preferred_element_type=jnp.float32)]
    reduce_sum x37 -> x0, other arithmetic: 104 us -> none  [the longest x3 50 us: layer_backward(): mix_value_grad = jnp.sum((1.0 - mix_rate)[:, :, None] * mix_grad, axis=0)]
    psum x1 -> x0, waiting for transfers between devices: 79.1 us -> none  [local(): lax.psum((query_weight_grad, key_weight_grad, value_weight_grad, out_weig...]
    all_to_all x11 -> x0, starting transfers between devices: 70.4 us -> none  [the longest x3 19.8 us: dispatch_grads(): lax.all_to_all(values, 'expert', split_axis=0, concat_axis=0, tiled=True)]
    psum x1 -> x0, blocking collectives: 54.6 us -> none  [local(): lax.psum((gain_one_grad, gain_two_grad, router_grad, residual_grad, mix_g...]
    unnamed x827 -> x22, local copies, waits for them, and re-layouts: 67.2 us -> 18.1 us
    gather x18 -> x0, local copies, waits for them, and re-layouts: 45.9 us -> none  [the longest x6 16.3 us: branches(): back_padded[destination].astype(jnp.float32)]
  transfers between devices with their start and end apart: 34 -> 0, of which waited for: 16 -> 0; matrix products, arithmetic and copies ran while one was open for 35% -> 0% of each run, Pallas kernels for 0% -> 0%
where the time goes in v1:
time: 509 us
  Pallas kernels  477 us (94%)
  local copies, waits for them, and re-layouts  22.9 us (4%)
  other arithmetic  7.79 us (2%)
    pallas_call x1, Pallas kernels, run_chain(): pl.pallas_call(functools.partial(chain_kernel, cfg, names), out_shape=[*o...  391 us
    pallas_call x1, Pallas kernels, run_tail(): pl.pallas_call(functools.partial(tail_kernel, cfg, names), out_shape=[*ou...  86.6 us
    unnamed x22, local copies, waits for them, and re-layouts  18.1 us

profile of v1, /device:TPU:10, one launch (start us, length us, event | category | flops | bytes accessed | tf_op | source)
XLA Modules:
  0.0 508.6 jit_solution(16790159945389424459)
XLA Ops:
  0.7 0.1 pad.16.clone
  0.7 0.7 reduce
  1.4 0.7 copy.55
  2.1 0.8 copy.54
  2.9 0.6 pad.9.refs_15_
  3.5 0.8 transpose_squeeze.4.refs_7_
  4.4 0.9 copy.43
  5.2 0.7 pad.8.refs_3_
  6.0 1.5 copy.44.refs_4_
  7.5 1.5 maximum_maximum_fusion.refs_14_
  9.0 390.6 %shard_map.324 = (f32[2,256,128]{2,1,0:T(8,128)}, f32[128,768]{1,0:T(8,128)}, f32[128,128]{1,0:T(8,128)}, f32[8,768]{1,0:T(8,128)}, f32[2,256,768]{2,1,0:T(8,128...) custom-call(s32[2,4]{1,0:T(2,128)} %bitcast.73, ...), custom_call_target="tpu_custom_call" | custom-call | flops 25367150592 | bytes 50000000 | tf_op jit(solution)/shard_map/pallas_call | solution.py:754
  399.7 1.0 slice_bitcast_fusion
  400.7 0.7 copy.46
  401.4 86.6 %shard_map.325 = (bf16[3200,384]{1,0:T(8,128)(2,1)}, f32[768,1024]{1,0:T(8,128)}, f32[768,1024]{1,0:T(8,128)}, f32[1024,768]{1,0:T(8,128)}) custom-call(bf16[2,512,768]{2,1,0:T(8,128)(2,1)} %get-tuple-element.40.refs_0_, bf16[2,512,768]{2,1,0:T(8,128)(2,1)} %get-tuple-element.41.refs_1_, bf16[2,512,384]{2,1,0:T(8,128)(2,1)} %get-tuple-element.42.refs_2_, ...), custom_call_target="tpu_custom_call" | custom-call | flops 9663676416 | bytes 40000000 | tf_op jit(solution)/shard_map/pallas_call | solution.py:1052
  488.0 0.9 slice_convert_fusion
  488.9 0.6 copy.49
  489.5 0.6 pad_maximum_fusion.2
  490.1 0.6 fusion
  490.7 0.7 copy.48
  491.4 3.5 convert_bitcast_fusion
  494.8 0.0 copy-start.4
  494.8 1.4 copy.47
  496.2 0.2 copy-done.4
  496.4 0.0 copy-start.3
  496.4 1.1 copy.61
  497.6 0.8 copy-done.3
  498.4 0.0 copy-start.2
  498.4 1.1 copy.62
  499.6 1.3 copy-done.2
  500.9 0.0 copy-start.1
  500.9 1.7 copy.63
  502.5 1.4 copy-done.1
  503.9 0.0 copy-start
  503.9 1.7 copy.64
  505.6 1.4 copy-done
  506.9 1.7 copy.65
  (5 shorter events, 0.0 us)
Async XLA Ops:
  494.8 1.6 copy-start.4
  496.4 2.0 copy-start.3
  498.4 2.5 copy-start.2
  500.9 3.0 copy-start.1
  503.9 3.0 copy-start

commit v2 on v1

--- a/solution.py
+++ b/solution.py
@@ -83,9 +83,8 @@
 
 def chain_kernel(cfg, names, *refs):
     r = types.SimpleNamespace(**dict(zip(names, refs, strict=True)))
-    owned, rows, experts, cap, cap_pad = cfg.owned, cfg.rows, cfg.experts, cfg.cap, cfg.cap_pad
-    choices, slots, tiles, tile_rows = cfg.choices, cfg.slots, cfg.tiles, cfg.tile_rows
-    per_tile, micro, sections, seqs = cfg.per_tile, cfg.micro, cfg.sections, cfg.seqs
+    owned, rows, experts, cap, slots = cfg.owned, cfg.rows, cfg.experts, cfg.cap, cfg.slots
+    choices, micro, sections, seqs = cfg.choices, cfg.micro, cfg.sections, cfg.seqs
     pairs, chunk = cfg.heads // 2, cfg.chunk
     scale = HEAD_DIM ** (-0.5)
     sec, me, core = (lax.axis_index(a) for a in ("section", "expert", "tensor"))
@@ -114,11 +113,46 @@
             device_id_type=MESH,
         )
 
+    main, rem, half_rows, rem_rows = cfg.main, cfg.rem, cfg.half_rows, cfg.rem_rows
+    rem_start = experts * main
+    group = experts // 2
+    my_group, in_group = me // group, lax.rem(me, group)
+    group_of = (my_group, 1 - my_group)
+
     def slot_rows(index):
-        return pl.ds(pl.multiple_of(index * cap_pad, cap_pad), cap_pad)
-
-    def tile_of(j):
-        return pl.ds(pl.multiple_of(j * tile_rows, tile_rows), tile_rows)
+        return pl.ds(pl.multiple_of(index * main, main), main)
+
+    def group_rows(g, offset=0):
+        return pl.ds(pl.multiple_of(offset + group_of[g] * half_rows, 16), half_rows)
+
+    def last_rows(offset=0):
+        return pl.ds(pl.multiple_of(offset + rem_start, 16), rem_rows)
+
+    def get(ref, g, offset=0, cols=slice(None)):
+        value = ref[group_rows(g, offset), cols]
+        if g == 1 and rem:
+            value = jnp.concatenate([value, ref[last_rows(offset), cols]], axis=0)
+        return value
+
+    def put(ref, g, value, offset=0, cols=slice(None)):
+        ref[group_rows(g, offset), cols] = value[:half_rows]
+        if g == 1 and rem:
+            ref[last_rows(offset), cols] = value[half_rows:]
+
+    pieces = -(-half_rows // 256)
+    hidden_cols = [
+        slice(k * cfg.inner // pieces, (k + 1) * cfg.inner // pieces) for k in range(pieces)
+    ]
+
+    def parts(g):
+        return [group_rows(g)] + ([last_rows()] if g == 1 and rem else [])
+
+    def peers_in(g, act):
+        def step(k, carry):
+            act(group_of[g] * group + lax.rem(in_group + k, group))
+            return carry
+
+        lax.fori_loop(1 - g, group, step, 0)
 
     def exchange(kind, m, peer, landed, source, target):
         return pltpu.make_async_remote_copy(
@@ -130,25 +164,45 @@
             device_id_type=MESH,
         )
 
-    def send_all(kind, m, source, target):
-        def step(k, carry):
-            exchange(kind, m, lax.rem(me + k, experts), me, source, target).start()
-            return carry
-
-        lax.fori_loop(1, experts, step, 0)
-
-    def wait_sent(kind, m, source, target):
-        def step(k, carry):
-            exchange(kind, m, lax.rem(me + k, experts), me, source, target).wait_send()
-            return carry
-
-        lax.fori_loop(1, experts, step, 0)
-
-    def wait_landed(kind, m, landed, source, target):
-        exchange(kind, m, landed, landed, source, target).wait_recv()
+    def exchange_rem(kind, m, peer, landed, source, target):
+        return pltpu.make_async_remote_copy(
+            src_ref=source.at[peer],
+            dst_ref=target.at[landed],
+            send_sem=r.rem_send.at[kind, m, peer],
+            recv_sem=r.rem_recv.at[kind, m, landed],
+            device_id={"expert": peer},
+            device_id_type=MESH,
+        )
+
+    def lay_rem(ref, value):
+        for k in range(rem):
+            ref[:, k, :] = value[k * experts : (k + 1) * experts]
+
+    def read_rem(ref):
+        value = [ref[:, k, :] for k in range(rem)]
+        rest = rem_rows - rem * experts
+        if rest:
+            value.append(jnp.zeros((rest, cfg.width), f32))
+        return jnp.concatenate(value, axis=0).astype(bf16)
+
+    def send_slots(kind, m, value):
+        r.outgoing[...] = value[:rem_start].astype(bf16)
+        mine = r.arrived.at[core]
+        for g in (1, 0):
+            peers_in(g, lambda p: exchange(kind, m, p, me, r.outgoing, mine).start())
+        if rem:
+            lay_rem(r.rem_out, value[rem_start:])
+            for g in (1, 0):
+                peers_in(g, lambda p: exchange_rem(kind, m, p, me, r.rem_out, r.rem_in).start())
+            r.rem_in[pl.ds(me, 1)] = r.rem_out[pl.ds(me, 1)]
+        r.arrived[core, slot_rows(me), :] = r.outgoing[slot_rows(me), :]
 
     def save(index, m, source, target):
         return pltpu.make_async_copy(source, target.at[m], r.local.at[index, m])
+
+    grad_back = r.inside.at[pl.ds(0, slots), pl.ds(0, cfg.width)]
+    back_hop = min(1, sections - 2)
+    stage = r.partial.at[pl.ds(0, owned)]
 
     barrier = pltpu.get_barrier_semaphore()
 
@@ -198,7 +252,7 @@
             piece = slice(c * chunk, (c + 1) * chunk)
             key = iota((chunk, rows), 1)
             seen = (key <= row[piece]) & (key >= start[piece])
-            r.bias[piece, :] = jnp.where(seen, 0.0, -1e30)
+            r.bias[piece, :] = jnp.where(seen, 0.0, -1e30).astype(bf16)
 
     def routing(m):
         lane = iota((owned, LANES), 1)
@@ -215,8 +269,14 @@
         for k in range(2):
             slot = jnp.sum(earlier * hot[k], axis=1, keepdims=True).astype(i32)
             slot_t = jnp.sum(earlier_t * hot_t[k], axis=0, keepdims=True).astype(i32)
-            place = jnp.where((col[k] < experts) & (slot < cap), col[k] * cap_pad + slot, -1)
-            place_t = jnp.where((row[k] < experts) & (slot_t < cap), row[k] * cap_pad + slot_t, -1)
+
+            def placed(choice, at):
+                first = choice * main + at
+                late = rem_start + (at - main) * experts + choice
+                kept = (choice < experts) & (at < cap)
+                return jnp.where(kept, jnp.where(at < main, first, late), -1)
+
+            place, place_t = placed(col[k], slot), placed(row[k], slot_t)
             r.place_col[m, :, k : k + 1] = place
             r.place_row[m, k : k + 1, :] = place_t
 
@@ -238,92 +298,87 @@
         pack = r.gates[m]
         return [pack[:, k : k + 1] for k in range(2)], [pack[:, 2 + k : 3 + k] for k in range(2)]
 
-    def through_expert(m, kind_in, kind_out, pair_in, pair_out, outgoing, arrived, target, kept, compute):
-        mine = arrived.at[core]
-        theirs = arrived.at[other]
-
-        def arrive(j, carry):
-            def one(k, inner):
-                source = j * per_tile + k
-
-                @pl.when(source != me)
-                def _():
-                    wait_landed(kind_in, m, source, outgoing, mine)
-
-                return inner
-
-            lax.fori_loop(0, per_tile, one, 0)
-            pair(pair_in, m, j, mine.at[tile_of(j)], mine.at[tile_of(j)]).start()
-            return carry
-
-        lax.fori_loop(0, tiles, arrive, 0)
-        passes = kind_in // 2
-
-        def keep(half, tile, j):
+    def through_expert(m, kind, pair_in, pair_out, target, kept, compute):
+        mine, theirs = r.arrived.at[core], r.arrived.at[other]
+        passes = kind // 2
+
+        def keep(index, half, rows_of):
             return pltpu.make_async_copy(
-                arrived.at[half, tile], kept.at[m, half, tile], r.keep.at[passes, m, half, j]
+                r.arrived.at[half, rows_of], kept.at[m, half, rows_of], r.keep.at[passes, m, index]
             )
 
-        def work(j, carry):
-            tile = tile_of(j)
-            keep(core, tile, j).start()
-            r.partial[tile, :] = compute(core, tile, 0, j)
-            pair(pair_in, m, j, theirs.at[tile], theirs.at[tile]).wait_recv()
-            keep(other, tile, j).start()
-            r.part_out[tile, :] = compute(other, tile, 1, j).astype(bf16)
-            keep(other, tile, j).wait()
-            pair(pair_out, m, j, r.part_out.at[tile], r.part_in.at[tile]).start()
-            return carry
-
-        lax.fori_loop(0, tiles, work, 0)
-
-        def read(j, carry):
-            tile = tile_of(j)
-            pair(pair_in, m, j, mine.at[tile], mine.at[tile]).wait_send()
-            keep(core, tile, j).wait()
-            return carry
-
-        lax.fori_loop(0, tiles, read, 0)
-
-        def finish(j, carry):
-            tile = tile_of(j)
-            pair(pair_out, m, j, r.part_out.at[tile], r.part_in.at[tile]).wait_recv()
-            r.result[tile, :] = (r.partial[tile, :] + wide(r.part_in[tile, :])).astype(bf16)
-
-            def one(k, inner):
-                source = j * per_tile + k
-
-                @pl.when(source != me)
-                def _():
-                    exchange(kind_out, m, source, me, r.result, target).start()
-
-                @pl.when(source == me)
-                def _():
-                    target[slot_rows(me), :] = r.result[slot_rows(me), :]
-
-                return inner
-
-            lax.fori_loop(0, per_tile, one, 0)
-            return carry
-
-        lax.fori_loop(0, tiles, finish, 0)
-
-        def done(j, carry):
-            tile = tile_of(j)
-            pair(pair_out, m, j, r.part_out.at[tile], r.part_in.at[tile]).wait_send()
-            return carry
-
-        lax.fori_loop(0, tiles, done, 0)
-        wait_sent(kind_in, m, outgoing, mine)
-
-    def wait_back(m, kind_out, target):
-
-        def one(k, carry):
-            wait_landed(kind_out, m, lax.rem(me + k, experts), r.result, target)
-            return carry
-
-        lax.fori_loop(1, experts, one, 0)
-        wait_sent(kind_out, m, r.result, target)
+        def forward_pair(g, which, side):
+            return [
+                pair(pair_in, m, g + k, side.at[rows_of], side.at[rows_of])
+                for k, rows_of in enumerate(parts(g))
+            ]
+
+        def sums(g):
+            return [
+                pair(pair_out, m, g + k, r.part_out.at[rows_of], r.part_in.at[rows_of])
+                for k, rows_of in enumerate(parts(g))
+            ]
+
+        everything = pl.ds(0, slots)
+        for g in range(2):
+            peers_in(g, lambda p: exchange(kind, m, p, p, r.outgoing, mine).wait_recv())
+            if g == 1 and rem:
+                for which in range(2):
+                    peers_in(which, lambda p: exchange_rem(kind, m, p, p, r.rem_out, r.rem_in).wait_recv())
+                r.arrived[core, last_rows(), :] = read_rem(r.rem_in)
+            for copy in forward_pair(g, core, mine):
+                copy.start()
+            kept_mine = [keep(2 * g + k, core, rows_of) for k, rows_of in enumerate(parts(g))]
+            for copy in kept_mine:
+                copy.start()
+            own = compute(core, g)
+            put(r.partial, g, own)
+            for copy in forward_pair(g, other, theirs):
+                copy.wait_recv()
+            if g == 1:
+                kept_theirs = keep(1, other, everything)
+                kept_theirs.start()
+            put(r.part_out, g, compute(other, g).astype(bf16))
+            if g == 1:
+                kept_theirs.wait()
+            for copy in sums(g):
+                copy.start()
+            for copy in sums(g):
+                copy.wait_recv()
+            value = get(r.partial, g) + wide(get(r.part_in, g))
+            for copy in kept_mine:
+                copy.wait()
+            for copy in forward_pair(g, core, mine):
+                copy.wait_send()
+            put(r.result, g, value.astype(bf16))
+            peers_in(g, lambda p: exchange(kind + 1, m, p, me, r.result, target).start())
+            if g == 1 and rem:
+                lay_rem(r.rem_result, value[half_rows:])
+                for which in (1, 0):
+                    peers_in(
+                        which,
+                        lambda p: exchange_rem(kind + 1, m, p, me, r.rem_result, r.rem_back).start(),
+                    )
+                r.rem_back[pl.ds(me, 1)] = r.rem_result[pl.ds(me, 1)]
+        target[slot_rows(me), :] = r.result[slot_rows(me), :]
+        for g in range(2):
+            for copy in sums(g):
+                copy.wait_send()
+            peers_in(g, lambda p: exchange(kind, m, p, me, r.outgoing, mine).wait_send())
+            if rem:
+                peers_in(g, lambda p: exchange_rem(kind, m, p, me, r.rem_out, r.rem_in).wait_send())
+
+    def wait_back(m, kind, target):
+        for g in range(2):
+            peers_in(g, lambda p: exchange(kind + 1, m, p, p, r.result, target).wait_recv())
+            if rem:
+                peers_in(g, lambda p: exchange_rem(kind + 1, m, p, p, r.rem_result, r.rem_back).wait_recv())
+        if rem:
+            target[last_rows(), :] = read_rem(r.rem_back)
+        for g in range(2):
+            peers_in(g, lambda p: exchange(kind + 1, m, p, me, r.result, target).wait_send())
+            if rem:
+                peers_in(g, lambda p: exchange_rem(kind + 1, m, p, me, r.rem_result, r.rem_back).wait_send())
 
     def forward(m, carry):
         @pl.when(is_first)
@@ -362,7 +417,7 @@
                 km, vm = k2 * keep, v2 * keep
                 for c in range(rows // chunk):
                     piece, reach = slice(c * chunk, (c + 1) * chunk), (c + 1) * chunk
-                    scores = dot_nt(q2[piece], km[:reach]) * scale + r.bias[piece, :reach]
+                    scores = dot_nt(q2[piece], km[:reach]) * scale + wide(r.bias[piece, :reach])
                     peak = jnp.max(scores, axis=-1, keepdims=True)
                     shifted = jnp.exp(scores - peak)
                     total = jnp.sum(shifted, axis=-1, keepdims=True)
@@ -389,11 +444,7 @@
         normed2 = (hidden * inverse_rms(hidden) * r.gain2[...]).astype(bf16)
         r.norm2[m] = normed2
 
-        into = r.arrived
-        both = spread_t(m, 0) + spread_t(m, 1)
-        r.outgoing[...] = dot(both, normed2).astype(bf16)
-        send_all(0, m, r.outgoing, into.at[core])
-        r.arrived[core, slot_rows(me), :] = r.outgoing[slot_rows(me), :]
+        send_slots(0, m, dot(spread_t(m, 0) + spread_t(m, 1), normed2))
 
         mixer_hi, mixer_lo = halves(r.mixer[...])
         logits = dot_nt(normed2, mixer_hi) + dot_nt(normed2, mixer_lo)
@@ -416,44 +467,32 @@
             for copy in weights:
                 copy.wait()
 
-        def compute(half, tile, slot, j):
-            block = r.arrived[half, tile, :]
-            place = pl.ds(pl.multiple_of(half * slots + tile.start, tile_rows), tile_rows)
-            value = dot(block, r.gate_v[...])
-            upper = dot(block, r.up_v[...])
-            sig = jax.nn.sigmoid(value)
-            active = value * sig
-            inside = (active * upper).astype(bf16)
-            r.by_up[place, :] = active.astype(bf16)
-            r.by_gate[place, :] = (upper * sig * (1.0 + value * (1.0 - sig))).astype(bf16)
-
-            def ring(at):
-                rows_of = pl.ds(pl.multiple_of(half * slots + at * tile_rows, tile_rows), tile_rows)
-                return pltpu.make_async_copy(
-                    r.inside.at[slot], r.h_inside.at[m, rows_of], r.ring.at[slot, m, at]
-                )
-
-            @pl.when(j > 0)
-            def _():
-                ring(j - 1).wait()
-
-            r.inside[slot] = inside
-            ring(j).start()
-
-            @pl.when(j == tiles - 1)
-            def _():
-                ring(j).wait()
-
-            return dot(inside, r.down_v[...])
-
-        through_expert(m, 0, 1, P_ROWS, P_PART, r.outgoing, into, r.back.at[m], r.h_rows, compute)
+        def compute(half, g):
+            block = get(r.arrived.at[half], g)
+            offset = half * slots
+            total = 0.0
+            for cols in hidden_cols:
+                value = dot(block, r.gate_v[:, cols])
+                upper = dot(block, r.up_v[:, cols])
+                sig = jax.nn.sigmoid(value)
+                active = value * sig
+                inside = (active * upper).astype(bf16)
+                put(r.by_up, g, active.astype(bf16), offset, cols)
+                slope = upper * sig * (1.0 + value * (1.0 - sig))
+                put(r.by_gate, g, slope.astype(bf16), offset, cols)
+                put(r.inside, g, inside, offset, cols)
+                total = total + dot(inside, r.down_v[cols, :])
+            return total
+
+        through_expert(m, 0, P_ROWS, P_PART, r.back.at[m], r.h_rows, compute)
         stored = [
+            save(10, m, r.inside, r.h_inside),
             save(5, m, r.by_up, r.h_up),
             save(6, m, r.by_gate, r.h_gate),
         ]
         for copy in stored:
             copy.start()
-        wait_back(m, 1, r.back.at[m])
+        wait_back(m, 0, r.back.at[m])
 
         apart = [dot(spread(m, k), r.back[m]) for k in range(2)]
         out = r.h[m] + gate[0] * apart[0] + gate[1] * apart[1]
@@ -463,8 +502,8 @@
             own = own + on * rate[c]
             out = out + (on * (1.0 - rate[c])) * r.const_value[c : c + 1, :]
         out = out + own * wide(r.norm2[m])
-        r.stage[...] = out
-        save(3, m, r.stage, r.layer_out).start()
+        stage[...] = out
+        save(3, m, stage, r.layer_out).start()
 
         @pl.when(sec < sections - 1)
         def _():
@@ -475,7 +514,7 @@
 
         pair(P_NORM, m, 0, r.norm.at[m, own_rows], r.norm.at[m, own_rows]).wait_send()
         pair(P_OUT, m, 0, r.half_out, r.half_in.at[0, m]).wait_send()
-        save(3, m, r.stage, r.layer_out).wait()
+        save(3, m, stage, r.layer_out).wait()
         save(1, m, r.norm.at[m], r.h_norm).wait()
         save(2, m, r.o.at[m], r.h_o).wait()
         for copy in stored:
@@ -504,16 +543,13 @@
 
         @pl.when(sec < sections - 1)
         def _():
-            hop(1, m, r.hop_out, r.hop_in.at[1, m], sec + 1).wait_recv()
-            r.dz[...] = wide(r.hop_in[1, m])
+            hop(1, m, r.hop_out, r.hop_in.at[back_hop, m], sec + 1).wait_recv()
+            r.dz[...] = wide(r.hop_in[back_hop, m])
 
         dz = r.dz[...]
         gate, rate = unpack_gates(m)
-        into = r.arrived
         leaving = [dot(spread_t(m, k), (gate[k] * dz).astype(bf16)) for k in range(2)]
-        r.outgoing[...] = (leaving[0] + leaving[1]).astype(bf16)
-        send_all(2, m, r.outgoing, into.at[core])
-        r.arrived[core, slot_rows(me), :] = r.outgoing[slot_rows(me), :]
+        send_slots(2, m, leaving[0] + leaving[1])
 
         col, copies, consts = choice_flags(m)
         normed2 = r.norm2[m]
@@ -548,27 +584,30 @@
         for copy in fetched:
             copy.wait()
 
-        def compute(half, tile, slot, j):
-            block = r.arrived[half, tile, :]
-            place = pl.ds(pl.multiple_of(half * slots + tile.start, tile_rows), tile_rows)
-            dinside = dot_nt(block, r.down_v[...])
-            dvalue = (dinside * wide(r.by_gate[place, :])).astype(bf16)
-            dupper = (dinside * wide(r.by_up[place, :])).astype(bf16)
-            r.by_gate[place, :] = dvalue
-            r.by_up[place, :] = dupper
-            return dot_nt(dvalue, r.gate_v[...]) + dot_nt(dupper, r.up_v[...])
-
-        through_expert(m, 2, 3, P_GROWS, P_GPART, r.outgoing, into, r.grad_back, r.h_grads, compute)
+        def compute(half, g):
+            block = get(r.arrived.at[half], g)
+            offset = half * slots
+            total = 0.0
+            for cols in hidden_cols:
+                dinside = dot_nt(block, r.down_v[cols, :])
+                dvalue = (dinside * wide(get(r.by_gate, g, offset, cols))).astype(bf16)
+                dupper = (dinside * wide(get(r.by_up, g, offset, cols))).astype(bf16)
+                put(r.by_gate, g, dvalue, offset, cols)
+                put(r.by_up, g, dupper, offset, cols)
+                total = total + dot_nt(dvalue, r.gate_v[:, cols]) + dot_nt(dupper, r.up_v[:, cols])
+            return total
+
+        through_expert(m, 2, P_GROWS, P_GPART, grad_back, r.h_grads, compute)
         stored = [
             save(11, m, r.by_up, r.h_up),
             save(12, m, r.by_gate, r.h_gate),
         ]
         for copy in stored:
             copy.start()
-        wait_back(m, 3, r.grad_back)
+        wait_back(m, 2, grad_back)
 
         both = spread(m, 0) + spread(m, 1)
-        dnorm = r.dnorm[...] + dot(both, r.grad_back[...])
+        dnorm = r.dnorm[...] + dot(both, grad_back[...])
         hidden = r.h[m]
         root = inverse_rms(hidden)
         scaled = dnorm * r.gain2[...]
@@ -594,7 +633,7 @@
                 km, vm, qm, dom = k2 * keep, v2 * keep, q2 * keep, do2 * keep
                 for c in range(rows // chunk):
                     piece, reach = slice(c * chunk, (c + 1) * chunk), (c + 1) * chunk
-                    scores = dot_nt(q2[piece], km[:reach]) * scale + r.bias[piece, :reach]
+                    scores = dot_nt(q2[piece], km[:reach]) * scale + wide(r.bias[piece, :reach])
                     total = jnp.sum(
                         jnp.where(head_lane == 2 * p + half, r.logsum[m, piece, :], 0.0),
                         axis=1,
@@ -643,12 +682,12 @@
         scaled1 = dnorm1 * r.gain1[...]
         pull1 = root1 * root1 * root1 * jnp.mean(x * scaled1, axis=-1, keepdims=True)
         dx = r.dh[...] + root1 * scaled1 - x * pull1
-        r.stage[...] = dx
-        save(4, m, r.stage, r.input_grad).start()
+        stage[...] = dx
+        save(4, m, stage, r.input_grad).start()
 
         @pl.when(sec > 0)
         def _():
-            copy = hop(1, m, r.hop_out, r.hop_in.at[1, m], sec - 1)
+            copy = hop(1, m, r.hop_out, r.hop_in.at[back_hop, m], sec - 1)
             r.hop_out[...] = dx.astype(bf16)
             copy.start()
             copy.wait_send()
@@ -656,7 +695,7 @@
         r.rows_grad[2:3, :] += jnp.sum(dnorm1 * x * root1, axis=0, keepdims=True)
         pair(P_DA, m, 0, r.da.at[own_rows], r.da.at[own_rows]).wait_send()
         pair(P_DX, m, 0, r.half_out, r.half_in.at[1, m]).wait_send()
-        save(4, m, r.stage, r.input_grad).wait()
+        save(4, m, stage, r.input_grad).wait()
         save_da.wait()
         for copy in stored + more:
             copy.wait()
@@ -694,6 +733,13 @@
         h_dv=shape((micro, rows, heads_width), bf16),
     )
     dma = pltpu.SemaphoreType.DMA
+    rem_scratch = {}
+    if cfg.rem:
+        last = pltpu.VMEM((cfg.experts, cfg.rem, width), f32)
+        rem_sem = dma((4, micro, cfg.experts))
+        rem_scratch = dict(
+            rem_out=last, rem_in=last, rem_result=last, rem_back=last, rem_send=rem_sem, rem_recv=rem_sem
+        )
     scratch = dict(
         gate_v=pltpu.VMEM((width, inner), bf16),
         up_v=pltpu.VMEM((width, inner), bf16),
@@ -710,24 +756,23 @@
         gates=pltpu.VMEM((micro, owned, LANES), f32),
         place_col=pltpu.VMEM((micro, owned, 2), i32),
         place_row=pltpu.VMEM((micro, 2, owned), i32),
-        bias=pltpu.VMEM((rows, rows), f32),
+        bias=pltpu.VMEM((rows, rows), bf16),
         arrived=pltpu.VMEM((2, slots, width), bf16),
         part_in=pltpu.VMEM((slots, width), bf16),
         back=pltpu.VMEM((micro, slots, width), bf16),
         half_in=pltpu.VMEM((2, micro, owned, width), bf16),
-        hop_in=pltpu.VMEM((2, micro, owned, width), bf16),
-        grad_back=pltpu.VMEM((slots, width), bf16),
-        outgoing=pltpu.VMEM((slots, width), bf16),
+        hop_in=pltpu.VMEM((min(2, cfg.sections - 1), micro, owned, width), bf16),
+        outgoing=pltpu.VMEM((cfg.experts * cfg.main, width), bf16),
         part_out=pltpu.VMEM((slots, width), bf16),
         result=pltpu.VMEM((slots, width), bf16),
-        partial=pltpu.VMEM((slots, width), f32),
+        partial=pltpu.VMEM((max(slots, owned), width), f32),
         half_out=pltpu.VMEM((owned, width), bf16),
         hop_out=pltpu.VMEM((owned, width), bf16),
-        inside=pltpu.VMEM((2, cfg.tile_rows, inner), bf16),
+        inside=pltpu.VMEM((2 * slots, inner), bf16),
+        **rem_scratch,
         by_up=pltpu.VMEM((2 * slots, inner), bf16),
         by_gate=pltpu.VMEM((2 * slots, inner), bf16),
         dz=pltpu.VMEM((owned, width), f32),
-        stage=pltpu.VMEM((owned, width), f32),
         dh=pltpu.VMEM((owned, width), f32),
         dnorm=pltpu.VMEM((owned, width), f32),
         da=pltpu.VMEM((rows, width), bf16),
@@ -738,15 +783,14 @@
         mix=pltpu.VMEM((rows, LANES), f32),
         mix_k=pltpu.VMEM((rows, LANES), f32),
         mix_v=pltpu.VMEM((rows, LANES), f32),
-        pair_send=dma((8, micro, cfg.tiles)),
-        pair_recv=dma((8, micro, cfg.tiles)),
+        pair_send=dma((8, micro, 3)),
+        pair_recv=dma((8, micro, 3)),
         hop_send=dma((2, micro)),
         hop_recv=dma((2, micro)),
         a2a_send=dma((4, micro, cfg.experts)),
         a2a_recv=dma((4, micro, cfg.experts)),
         local=dma((17, micro)),
-        keep=dma((2, micro, 2, cfg.tiles)),
-        ring=dma((2, micro, cfg.tiles)),
+        keep=dma((2, micro, 4)),
         fetch=dma((3,)),
     )
     names = [*ins, *outs, *hbm_outs, *scratch]
@@ -1102,8 +1146,10 @@
     experts = choices - 4
     assert experts == peers and tensors == 2
     cap = 9 * 2 * owned // (8 * choices) + 1
-    cap_pad = -(-cap // 16) * 16
-    per_tile = max(d for d in range(1, peers + 1) if peers % d == 0 and d * cap_pad <= 256)
+    main, rem = cap // 16 * 16, cap % 16
+    if rem > 2 or not main:
+        main, rem = main + (16 if rem else 0), 0
+    rem_rows = -(-rem * peers // 16) * 16
     cfg = types.SimpleNamespace(
         micro=micro,
         owned=owned,
@@ -1114,11 +1160,11 @@
         experts=experts,
         choices=choices,
         cap=cap,
-        cap_pad=cap_pad,
-        slots=peers * cap_pad,
-        per_tile=per_tile,
-        tiles=peers // per_tile,
-        tile_rows=per_tile * cap_pad,
+        main=main,
+        rem=rem,
+        rem_rows=rem_rows,
+        half_rows=peers // 2 * main,
+        slots=peers * main + rem_rows,
         sections=lax.axis_size("section"),
         seqs=lengths.shape[2] - 1,
         chunk=owned,

time: 509 us -> 483 us (0.949)
  Pallas kernels: 477 us -> 446 us
    pallas_call x1, Pallas kernels: 391 us -> 361 us  [run_chain(): pl.pallas_call(functools.partial(chain_kernel, cfg, names), out_shape=[*o...]
where the time goes in v2:
time: 483 us; the launch traced here: 478 us
  Pallas kernels  446 us (92%)
  local copies, waits for them, and re-layouts  22.9 us (5%)
  other arithmetic  7.79 us (2%)
    pallas_call x1, Pallas kernels, run_chain(): pl.pallas_call(functools.partial(chain_kernel, cfg, names), out_shape=[*o...  361 us
    pallas_call x1, Pallas kernels, run_tail(): pl.pallas_call(functools.partial(tail_kernel, cfg, names), out_shape=[*ou...  85.1 us
    unnamed x22, local copies, waits for them, and re-layouts  18.1 us

profile of v2, /device:TPU:10, one launch (start us, length us, event | category | flops | bytes accessed | tf_op | source)
XLA Modules:
  0.0 477.9 jit_solution(4945038969727429324)
XLA Ops:
  0.7 0.1 pad.16.clone
  0.7 0.7 reduce
  1.4 0.7 copy.55
  2.1 0.8 copy.54
  2.9 0.6 pad.9.refs_15_
  3.5 0.8 transpose_squeeze.4.refs_7_
  4.4 0.9 copy.43
  5.2 0.7 pad.8.refs_3_
  6.0 1.5 copy.44.refs_4_
  7.5 1.5 maximum_maximum_fusion.refs_14_
  9.0 361.3 %shard_map.324 = (f32[2,256,128]{2,1,0:T(8,128)}, f32[128,768]{1,0:T(8,128)}, f32[128,128]{1,0:T(8,128)}, f32[8,768]{1,0:T(8,128)}, f32[2,256,768]{2,1,0:T(8,128...) custom-call(s32[2,4]{1,0:T(2,128)} %bitcast.73, ...), custom_call_target="tpu_custom_call" | custom-call | flops 21139292160 | bytes 50000000 | tf_op jit(solution)/shard_map/pallas_call | solution.py:798
  370.3 1.0 slice_bitcast_fusion
  371.3 0.7 copy.46
  372.0 85.1 %shard_map.325 = (bf16[3200,384]{1,0:T(8,128)(2,1)}, f32[768,1024]{1,0:T(8,128)}, f32[768,1024]{1,0:T(8,128)}, f32[1024,768]{1,0:T(8,128)}) custom-call(bf16[2,512,768]{2,1,0:T(8,128)(2,1)} %get-tuple-element.40.refs_0_, bf16[2,512,768]{2,1,0:T(8,128)(2,1)} %get-tuple-element.41.refs_1_, bf16[2,512,384]{2,1,0:T(8,128)(2,1)} %get-tuple-element.42.refs_2_, ...), custom_call_target="tpu_custom_call" | custom-call | flops 7549747200 | bytes 40000000 | tf_op jit(solution)/shard_map/pallas_call | solution.py:1096
  457.1 0.9 slice_convert_fusion
  458.0 0.6 copy.49
  458.6 0.6 pad_maximum_fusion.2
  459.2 0.6 fusion
  459.8 0.7 copy.48
  460.5 3.5 convert_bitcast_fusion
  464.0 0.0 copy-start.4
  464.0 1.4 copy.47
  465.3 0.2 copy-done.4
  465.6 0.0 copy-start.3
  465.6 1.1 copy.61
  466.7 0.8 copy-done.3
  467.6 0.0 copy-start.2
  467.6 1.1 copy.62
  468.7 1.3 copy-done.2
  470.0 0.0 copy-start.1
  470.0 1.7 copy.63
  471.7 1.4 copy-done.1
  473.0 0.0 copy-start
  473.0 1.7 copy.64
  474.7 1.4 copy-done
  476.1 1.7 copy.65
  (5 shorter events, 0.0 us)
Async XLA Ops:
  464.0 1.6 copy-start.4
  465.6 2.0 copy-start.3
  467.6 2.5 copy-start.2
  470.0 3.0 copy-start.1
  473.0 3.0 copy-start
